TPU v7x, 128 devices: a whole 4x4x4 slice. The times are simulated.
128 devices in a mesh: ctx: 32 (over z, y_hi, x), fsdp: 4 (over y_lo, core).
Axes of the slice: x: 4, y: 4 (y_hi: 2, y_lo: 2; y = y_hi * 2 + y_lo), z: 4, core: 2. Of those that a mesh axis runs over, the one named last changes fastest.
Arguments:
- tokens: bfloat16 [4, 4096, 960], P('fsdp', 'ctx'), may hold values from -6 to 6
- cotangent: bfloat16 [4, 4096, 960], P('fsdp', 'ctx'), may hold values from -6 to 6
- block_table: int32 [64], replicated, may hold values from 0 to 63, as said below
- attn_gain: bfloat16 [960], P('fsdp'), may hold values from 0.5 to 1.5
- w_query: bfloat16 [960, 960], P('fsdp'), may hold values from -0.1875 to 0.1875
- w_key: bfloat16 [960, 320], P('fsdp'), may hold values from -0.1875 to 0.1875
- w_value: bfloat16 [960, 320], P('fsdp'), may hold values from -0.1875 to 0.1875
- w_out: bfloat16 [960, 960], P('fsdp'), may hold values from -1 to 1
- mlp_gain: bfloat16 [960], P('fsdp'), may hold values from 0.5 to 1.5
- w_gate: bfloat16 [960, 2560], P('fsdp'), may hold values from -0.1875 to 0.1875
- w_up: bfloat16 [960, 2560], P('fsdp'), may hold values from -0.1875 to 0.1875
- w_down: bfloat16 [2560, 960], P('fsdp'), may hold values from -0.125 to 0.125
Outputs:
- layer_out: bfloat16 [4, 4096, 960], P('fsdp', 'ctx')
- grad_tokens: float32 [4, 4096, 960], P('fsdp', 'ctx')
- grad_attn_gain: float32 [960], P('fsdp')
- grad_query: float32 [960, 960], P('fsdp')
- grad_key: float32 [960, 320], P('fsdp')
- grad_value: float32 [960, 320], P('fsdp')
- grad_out: float32 [960, 960], P('fsdp')
- grad_mlp_gain: float32 [960], P('fsdp')
- grad_gate: float32 [960, 2560], P('fsdp')
- grad_up: float32 [960, 2560], P('fsdp')
- grad_down: float32 [2560, 960], P('fsdp')
Inputs may be any that keep to these rules, and one draw needn't show every extreme that they name: `block_table`: entries 2c and 2c + 1 are the numbers of the two blocks of 64 positions held by index c of ctx, in the order of its rows; every block number appears once, and the two numbers of one index sum to 63.
All inputs are finite; a program needn't handle non-finite values.
Results may differ from a plain program's by a relative error of at most 0.034.
Values may be sent and summed in bfloat16 or wider, within the bound.
A program may use at most 192 MiB of HBM per device.

v0:
```python
import jax
import jax.numpy as jnp
from jax import lax
from jax.sharding import PartitionSpec as P

HEADS = 15
KV_HEADS = 5
HEAD = 64


EPSILON = 1e-05
BASE = 10000.0


def sent_together(arrays, axis, dim, along):
    columns = [a.reshape(*a.shape[:along], -1) for a in arrays]
    both = jnp.concatenate(columns, axis=along)
    result, at, done = (lax.all_gather(both, axis, axis=dim, tiled=True), 0, [])
    for a, column in zip(arrays, columns):
        piece = result[..., at : at + column.shape[along]]
        done.append(piece.reshape(*piece.shape[:along], *a.shape[along:]))
        at += column.shape[along]
    return tuple(done)


def sent_together_2(arrays, axis, dim, along):
    ends, at = ([], 0)
    for a in arrays[:-1]:
        at += a.shape[along]
        ends.append(at)
    both = jnp.concatenate(arrays, axis=along)
    return tuple(
        jnp.split(lax.psum_scatter(both, axis, scatter_dimension=dim, tiled=True), ends, axis=along)
    )


def together(arrays, axis):
    ravelled, at, done = (jnp.concatenate([a.reshape(-1) for a in arrays]), 0, [])
    subtotal = lax.psum(ravelled, axis)
    for a in arrays:
        done.append(subtotal[at : at + a.size].reshape(a.shape))
        at += a.size
    return tuple(done)


def norm_forward(value_matrix, gain):
    inv_rms = lax.rsqrt(jnp.mean(value_matrix * value_matrix, axis=-1, keepdims=True) + EPSILON)
    return (value_matrix * inv_rms * gain, inv_rms)


def norm_backward(value_matrix, inv_rms, gain, grad_normed):
    scaled = grad_normed * gain
    grad_values = inv_rms * scaled - value_matrix * inv_rms * inv_rms * inv_rms * jnp.mean(
        scaled * value_matrix, axis=-1, keepdims=True
    )
    grad_gain = jnp.sum(grad_normed * value_matrix * inv_rms, axis=0)
    return (grad_values, grad_gain)


def rope_tables(positions, half_dim):
    frequency = BASE ** (-jnp.arange(half_dim, dtype=jnp.float32) / half_dim)
    angles = positions.astype(jnp.float32)[:, None] * frequency[None, :]
    cosine = jnp.concatenate([jnp.cos(angles), jnp.cos(angles)], axis=-1)[:, None, :]
    sine_table = jnp.concatenate([jnp.sin(angles), jnp.sin(angles)], axis=-1)[:, None, :]
    return (cosine, sine_table)


def rotate(value_matrix, cosine, sine_table):
    half_dim = value_matrix.shape[-1] // 2
    turned = jnp.concatenate([-value_matrix[..., half_dim:], value_matrix[..., :half_dim]], axis=-1)
    return value_matrix * cosine + turned * sine_table


def outer_sum(left_operand, right_operand):
    return lax.dot_general(
        left_operand, right_operand, (((0,), (0,)), ((), ())), preferred_element_type=jnp.float32
    )


def back_dot(grad_rows, weight):
    return lax.dot_general(
        grad_rows, weight, (((1,), (1,)), ((), ())), preferred_element_type=jnp.float32
    )


def block_scores(query_matrix, block_of_keys, key_pos, query_pos, score_scale):
    logit_scores = (
        jnp.einsum(
            "kmcu,nmu->mckn", query_matrix, block_of_keys, preferred_element_type=jnp.float32
        )
        * score_scale
    )
    allowed = key_pos[None, :] <= query_pos[:, None]
    return jnp.where(allowed[None, None], logit_scores, -1e30)


def on_device(
    tokens,
    cotangent,
    block_table,
    attn_gain,
    w_query,
    w_key,
    w_value,
    w_out,
    mlp_gain,
    w_gate,
    w_up,
    w_down,
):
    tok_rows = tokens.shape[1]
    model_width = tokens.shape[2]
    group = HEADS // KV_HEADS
    score_scale = HEAD ** (-0.5)
    ctx_count = lax.axis_size("ctx")
    block_rows = tok_rows // 2
    length = tok_rows * ctx_count
    key_rows = min(length, 1024)
    key_count = length // key_rows
    gain_a_low, query_w, key_w, value_w, out_w, gain_b_low, gate_w, up_w, down_w = (
        *sent_together(
            (attn_gain, w_query, w_key, w_value, w_out, mlp_gain, w_gate, w_up), "fsdp", 0, 1
        ),
        lax.all_gather(w_down, "fsdp", axis=0, tiled=True),
    )
    offsets = jnp.arange(block_rows, dtype=jnp.int32)
    own_blocks = lax.dynamic_slice_in_dim(block_table, 2 * lax.axis_index("ctx"), 2)
    local_pos = (own_blocks[:, None] * block_rows + offsets[None, :]).reshape(tok_rows)
    all_pos = (block_table[:, None] * block_rows + offsets[None, :]).reshape(length)
    cosine, sine_table = rope_tables(local_pos, HEAD // 2)
    resid_in = tokens[0].astype(jnp.float32)
    gain_a = gain_a_low.astype(jnp.float32)
    normed_a, inv_a = norm_forward(resid_in, gain_a)
    normed_a_low = normed_a.astype(jnp.bfloat16)
    query_pre = jnp.dot(normed_a_low, query_w, preferred_element_type=jnp.float32)
    key_pre = jnp.dot(normed_a_low, key_w, preferred_element_type=jnp.float32)
    value_low = jnp.dot(normed_a_low, value_w, preferred_element_type=jnp.float32).astype(
        jnp.bfloat16
    )
    query_matrix = rotate(query_pre.reshape(tok_rows, HEADS, HEAD), cosine, sine_table).astype(
        jnp.bfloat16
    )
    query_matrix = query_matrix.reshape(tok_rows, KV_HEADS, group, HEAD)
    keys_low = rotate(key_pre.reshape(tok_rows, KV_HEADS, HEAD), cosine, sine_table).astype(
        jnp.bfloat16
    )
    keys_low = keys_low.reshape(tok_rows, KV_HEADS * HEAD)
    keys_all, values_all = (
        lax.all_gather(keys_low, "ctx", axis=0, tiled=True),
        lax.all_gather(value_low, "ctx", axis=0, tiled=True),
    )
    key_blocks = keys_all.reshape(key_count, key_rows, KV_HEADS, HEAD)
    value_blocks = values_all.reshape(key_count, key_rows, KV_HEADS, HEAD)
    pos_blocks = all_pos.reshape(key_count, key_rows)

    def stats_step(carry, inputs):
        run_max, run_sum = carry
        block_of_keys, key_pos = inputs
        logit_scores = block_scores(query_matrix, block_of_keys, key_pos, local_pos, score_scale)
        new_max = jnp.maximum(run_max, jnp.max(logit_scores, axis=-1))
        run_sum = run_sum * jnp.exp(run_max - new_max) + jnp.sum(
            jnp.exp(logit_scores - new_max[..., None]), axis=-1
        )
        return ((new_max, run_sum), None)

    start_max = jnp.full((KV_HEADS, group, tok_rows), -1e30, jnp.float32)
    start_sum = jnp.zeros((KV_HEADS, group, tok_rows), jnp.float32)
    (row_max, row_sum), _ = lax.scan(stats_step, (start_max, start_sum), (key_blocks, pos_blocks))
    log_sum = row_max + jnp.log(row_sum)

    def output_step(total_out, inputs):
        block_of_keys, block_of_values, key_pos = inputs
        prob_block = jnp.exp(
            block_scores(query_matrix, block_of_keys, key_pos, local_pos, score_scale)
            - log_sum[..., None]
        )
        part_out = jnp.einsum(
            "cxfz,zcq->fcxq",
            prob_block.astype(jnp.bfloat16),
            block_of_values,
            preferred_element_type=jnp.float32,
        )
        return (total_out + part_out, None)

    start_out = jnp.zeros((tok_rows, KV_HEADS, group, HEAD), jnp.float32)
    attention_output, _ = lax.scan(output_step, start_out, (key_blocks, value_blocks, pos_blocks))
    attended_low = attention_output.reshape(tok_rows, HEADS * HEAD).astype(jnp.bfloat16)
    middle = resid_in + jnp.dot(attended_low, out_w, preferred_element_type=jnp.float32)
    gain_b = gain_b_low.astype(jnp.float32)
    normed_b, inv_b = norm_forward(middle, gain_b)
    normed_b_low = normed_b.astype(jnp.bfloat16)
    gate_pre = jnp.dot(normed_b_low, gate_w, preferred_element_type=jnp.float32)
    up_pre = jnp.dot(normed_b_low, up_w, preferred_element_type=jnp.float32)
    sigmoid_gate = jax.nn.sigmoid(gate_pre)
    silu_gate = gate_pre * sigmoid_gate
    hidden_low = (silu_gate * up_pre).astype(jnp.bfloat16)
    layer_out = middle + jnp.dot(hidden_low, down_w, preferred_element_type=jnp.float32)
    grad_low = cotangent[0]
    grad_down = outer_sum(hidden_low, grad_low)
    grad_hidden = back_dot(grad_low, down_w)
    grad_gate_pre = (
        grad_hidden * up_pre * sigmoid_gate * (1.0 + gate_pre * (1.0 - sigmoid_gate))
    ).astype(jnp.bfloat16)
    grad_up_pre = (grad_hidden * silu_gate).astype(jnp.bfloat16)
    grad_gate = outer_sum(normed_b_low, grad_gate_pre)
    grad_up = outer_sum(normed_b_low, grad_up_pre)
    grad_norm_b = back_dot(grad_gate_pre, gate_w) + back_dot(grad_up_pre, up_w)
    grad_mid_norm, grad_gain_b = norm_backward(middle, inv_b, gain_b, grad_norm_b)
    grad_middle = grad_low.astype(jnp.float32) + grad_mid_norm
    grad_branch = grad_middle.astype(jnp.bfloat16)
    grad_out = outer_sum(attended_low, grad_branch)
    grad_attention_output = (
        back_dot(grad_branch, out_w).astype(jnp.bfloat16).reshape(tok_rows, KV_HEADS, group, HEAD)
    )
    row_correction = jnp.einsum(
        "mqon,mqon->qom", grad_attention_output.astype(jnp.float32), attention_output
    )
    keys_back, values_back = (
        lax.all_gather(keys_low, "ctx", axis=0, tiled=True),
        lax.all_gather(value_low, "ctx", axis=0, tiled=True),
    )
    key_blocks = keys_back.reshape(key_count, key_rows, KV_HEADS, HEAD)
    value_blocks = values_back.reshape(key_count, key_rows, KV_HEADS, HEAD)

    def grad_step(grad_queries, inputs):
        block_of_keys, block_of_values, key_pos = inputs
        prob_block = jnp.exp(
            block_scores(query_matrix, block_of_keys, key_pos, local_pos, score_scale)
            - log_sum[..., None]
        )
        grad_probs = jnp.einsum(
            "kmcu,nmu->mckn",
            grad_attention_output,
            block_of_values,
            preferred_element_type=jnp.float32,
        )
        grad_score_matrix = (prob_block * (grad_probs - row_correction[..., None])).astype(
            jnp.bfloat16
        )
        grad_queries = grad_queries + jnp.einsum(
            "cxfz,zcq->fcxq", grad_score_matrix, block_of_keys, preferred_element_type=jnp.float32
        )
        grad_key_block = jnp.einsum(
            "khvu,vkhf->ukf", grad_score_matrix, query_matrix, preferred_element_type=jnp.float32
        )
        grad_value_block = jnp.einsum(
            "khvu,vkhf->ukf",
            prob_block.astype(jnp.bfloat16),
            grad_attention_output,
            preferred_element_type=jnp.float32,
        )
        return (grad_queries, (grad_key_block, grad_value_block))

    grad_queries, (grad_key_blocks, grad_value_blocks) = lax.scan(
        grad_step, start_out, (key_blocks, value_blocks, pos_blocks)
    )
    grad_keys_part = grad_key_blocks.reshape(length, KV_HEADS * HEAD) * score_scale
    grad_values_part = grad_value_blocks.reshape(length, KV_HEADS * HEAD)
    grad_keys, grad_values = tuple(
        (
            part.astype(jnp.float32)
            for part in sent_together_2(
                (grad_keys_part.astype(jnp.bfloat16), grad_values_part.astype(jnp.bfloat16)),
                "ctx",
                0,
                1,
            )
        )
    )
    grad_value_low = grad_values.astype(jnp.bfloat16)
    grad_key_pre = rotate(grad_keys.reshape(tok_rows, KV_HEADS, HEAD), cosine, -sine_table)
    grad_key_pre = grad_key_pre.reshape(tok_rows, KV_HEADS * HEAD).astype(jnp.bfloat16)
    grad_query_pre = rotate(
        (grad_queries * score_scale).reshape(tok_rows, HEADS, HEAD), cosine, -sine_table
    )
    grad_query_pre = grad_query_pre.reshape(tok_rows, HEADS * HEAD).astype(jnp.bfloat16)
    grad_query = outer_sum(normed_a_low, grad_query_pre)
    grad_key = outer_sum(normed_a_low, grad_key_pre)
    grad_value = outer_sum(normed_a_low, grad_value_low)
    grad_norm_a = (
        back_dot(grad_query_pre, query_w)
        + back_dot(grad_key_pre, key_w)
        + back_dot(grad_value_low, value_w)
    )
    grad_in_norm, grad_gain_a = norm_backward(resid_in, inv_a, gain_a, grad_norm_a)
    grad_tokens = grad_middle + grad_in_norm
    shard_q, shard_k, shard_v, shard_o, shard_g, shard_u, shard_d = (
        *tuple(
            (
                part.astype(jnp.float32)
                for part in sent_together_2(
                    (
                        grad_query.astype(jnp.bfloat16),
                        grad_key.astype(jnp.bfloat16),
                        grad_value.astype(jnp.bfloat16),
                        grad_out.astype(jnp.bfloat16),
                        grad_gate.astype(jnp.bfloat16),
                        grad_up.astype(jnp.bfloat16),
                    ),
                    "fsdp",
                    0,
                    1,
                )
            )
        ),
        lax.psum_scatter(
            grad_down.astype(jnp.bfloat16), "fsdp", scatter_dimension=0, tiled=True
        ).astype(jnp.float32),
    )
    shard_q, shard_k, shard_v, shard_o, shard_g, shard_u, shard_d = tuple(
        (
            part.astype(jnp.float32)
            for part in together(
                (
                    shard_q.astype(jnp.bfloat16),
                    shard_k.astype(jnp.bfloat16),
                    shard_v.astype(jnp.bfloat16),
                    shard_o.astype(jnp.bfloat16),
                    shard_g.astype(jnp.bfloat16),
                    shard_u.astype(jnp.bfloat16),
                    shard_d.astype(jnp.bfloat16),
                ),
                "ctx",
            )
        )
    )
    total_gain_a, total_gain_b = together((grad_gain_a, grad_gain_b), ("ctx", "fsdp"))
    gain_rows = model_width // lax.axis_size("fsdp")
    gain_start = lax.axis_index("fsdp") * gain_rows
    shard_gain_a = lax.dynamic_slice_in_dim(total_gain_a, gain_start, gain_rows)
    shard_gain_b = lax.dynamic_slice_in_dim(total_gain_b, gain_start, gain_rows)
    return (
        layer_out.astype(jnp.bfloat16)[None],
        grad_tokens[None],
        shard_gain_a,
        shard_q,
        shard_k,
        shard_v,
        shard_o,
        shard_gain_b,
        shard_g,
        shard_u,
        shard_d,
    )


def solution(mesh):
    return jax.shard_map(
        on_device,
        mesh=mesh,
        in_specs=(
            P("fsdp", "ctx", None),
            P("fsdp", "ctx", None),
            P(),
            P("fsdp"),
            P("fsdp", None),
            P("fsdp", None),
            P("fsdp", None),
            P("fsdp", None),
            P("fsdp"),
            P("fsdp", None),
            P("fsdp", None),
            P("fsdp", None),
        ),
        out_specs=(
            P("fsdp", "ctx", None),
            P("fsdp", "ctx", None),
            P("fsdp"),
            P("fsdp", None),
            P("fsdp", None),
            P("fsdp", None),
            P("fsdp", None),
            P("fsdp"),
            P("fsdp", None),
            P("fsdp", None),
            P("fsdp", None),
        ),
        check_vma=False,
    )
```

profile of v0, /device:TPU:1, one launch (start us, length us, event | category | flops | bytes accessed | tf_op | source)
XLA Modules:
  0.0 1360.7 jit_solution(9365995123682844608)
XLA Ops:
  10.9 7.7 concatenate.39
  19.6 139.1 %all-gather.5.cloned.1.call-done = bf16[960,7682]{1,0:T(8,128)(2,1)} async-done(((bf16[240,7682]{1,0:T(8,128)(2,1)}), bf16[960,7682]{1,0:T(8,128)(2,1)}) %all-gather.5.cloned.1.call-update) | async-done | bytes 14749456 | tf_op jit(solution)/shard_map/all_gather | solution.py:18
  160.1 2.9 convolution_convert_fusion.7
  167.7 46.1 %all-gather.11.cloned.1.call-done = bf16[2560,960]{0,1:T(8,128)(2,1)} async-done(((bf16[640,960]{0,1:T(8,128)(2,1)}), bf16[2560,960]{0,1:T(8,128)(2,1)}) %all-gather.11.cloned.1.call-update) | async-done | bytes 4915216 | tf_op jit(solution)/shard_map/all_gather | solution.py:124
  213.8 4.3 fusion.124
  218.2 3.8 slice_bitcast_fusion
  225.8 63.3 %all-gather.7.cloned.1.call-done = bf16[4096,320]{0,1:T(8,128)(2,1)} async-done(((bf16[128,320]{0,1:T(8,128)(2,1)}), bf16[4096,320]{0,1:T(8,128)(2,1)}) %all-gather.7.cloned.1.call-update) | async-done | bytes 2621456 | tf_op jit(solution)/shard_map/all_gather | solution.py:150
  289.0 4.3 reshape.420
  295.7 68.1 %all-gather.9.cloned.1.call-done = bf16[4096,320]{0,1:T(8,128)(2,1)} async-done(((bf16[128,320]{0,1:T(8,128)(2,1)}), bf16[4096,320]{0,1:T(8,128)(2,1)}) %all-gather.9.cloned.1.call-update) | async-done | bytes 2621456 | tf_op jit(solution)/shard_map/all_gather | solution.py:149
  363.8 5.5 reshape.422
  371.9 38.8 %while.39 = (s32[]{:T(128)}, f32[5,3,128]{2,1,0:T(4,128)S(1)}, f32[5,3,128]{2,1,0:T(4,128)S(1)}, s32[4,1024]{1,0:T(4,128)S(1)}, bf16[4,1024,5,64]{1,3,2,0:T(8,12...) while((s32[]{:T(128)}, f32[5,3,128]{2,1,0:T(4,128)S(1)}, ...), condition=%wide.region_4.5_spmd.clone, body=%wide.region_1.4_spmd.clone.sunk | while | flops 265561600 | bytes 17137280 | solution.py:168
  372.3 4.4 fusion.201
  376.7 4.8 exponential_reduce_fusion.2
  382.0 4.4 fusion.201
  386.4 4.8 exponential_reduce_fusion.2
  391.7 4.4 fusion.201
  396.1 4.8 exponential_reduce_fusion.2
  401.4 4.4 fusion.201
  405.8 4.8 exponential_reduce_fusion.2
  410.7 19.5 %while.40 = (s32[]{:T(128)}, f32[128,5,3,64]{0,3,2,1:T(8,128)}, bf16[4,1024,5,64]{1,3,2,0:T(8,128)(2,1)}, s32[4,1024]{1,0:T(4,128)S(1)}, bf16[4,1024,5,64]{1,3,2...) while((s32[]{:T(128)}, f32[128,5,3,64]{0,3,2,1:T(8,128)}, ...), condition=%wide.region_6.7_spmd.clone, body=%wide.region_5.6_spmd.clone.sunk | while | flops 511557760 | bytes 2827906 | solution.py:186
  411.1 4.4 fusion.207
  415.8 4.5 fusion.207
  420.7 4.5 fusion.207
  425.6 4.5 fusion.207
  431.4 3.7 multiply_reduce_fusion.2
  435.3 4.5 fusion.66
  439.8 5.7 multiply_convert_fusion.2
  445.5 5.0 fusion.64
  450.5 4.6 multiply_reduce_fusion
  459.4 99.5 %while.41 = (s32[]{:T(128)}, f32[128,5,3,64]{0,3,2,1:T(8,128)S(1)}, f32[4,1024,5,64]{1,3,2,0:T(8,128)}, bf16[4,1024,5,64]{1,3,2,0:T(8,128)(2,1)}, bf16[4,1024,5,...) while((s32[]{:T(128)}, f32[128,5,3,64]{0,3,2,1:T(8,128)S(1)}, ...), condition=%wide.region_10.11_spmd.clone, body=%wide.region_9.10_spmd.clone.sunk | while | flops 1278328960 | bytes 95788320 | solution.py:254
  459.8 4.4 fusion.218
  464.5 8.0 fusion.219
  472.5 3.1 fusion.220
  475.6 5.3 fusion.221
  484.5 4.4 fusion.218
  489.2 8.0 fusion.219
  497.2 3.1 fusion.220
  500.3 5.4 fusion.221
  509.3 4.4 fusion.218
  514.0 8.0 fusion.219
  522.0 3.1 fusion.220
  525.1 5.3 fusion.221
  534.0 4.4 fusion.218
  538.7 8.0 fusion.219
  546.7 3.1 fusion.220
  549.8 5.3 fusion.221
  558.9 3.9 copy.75
  570.6 7.9 copy.100
  579.7 3.7 convolution_convert_fusion
  583.3 7.9 copy.102
  595.7 3.6 convolution_convert_fusion.2
  599.3 3.6 convolution_convert_fusion.1
  602.9 148.2 %reduce-scatter.10.cloned.1.call-done = bf16[128,640]{1,0:T(8,128)(2,1)} async-done(((bf16[4096,640]{1,0:T(8,128)(2,1)}), bf16[128,640]{1,0:T(8,128)(2,1)}) %reduce-scatter.10.cloned.1.call-update) | async-done | bytes 163856
  759.6 22.3 %concatenate.49 = bf16[960,7680]{1,0:T(8,128)(2,1)} concatenate(bf16[960,960]{1,0:T(8,128)(2,1)S(1)} %convolution_convert_fusion.4, bf16[960,320]{1,0:T(8,128)(2,1)S(1)} %copy.76, bf16[960,320]{1,0:T(8,128)(2,1)} %copy.77, bf16[960,960]{1,0:T(8,128)(2,1)} %convolution_convert_fusion.3, bf16[960,2560]{1,0:T(8,128)(2,1)} %convolution_convert_fusion.2, ...), dimensions={1} | concatenate | bytes 29491200 | tf_op jit(solution)/shard_map/concatenate | solution.py:31
  782.3 42.5 %reduce-scatter.12.cloned.1.call-done = bf16[640,960]{1,0:T(8,128)(2,1)} async-done(((bf16[2560,960]{1,0:T(8,128)(2,1)}), bf16[640,960]{1,0:T(8,128)(2,1)}) %reduce-scatter.12.cloned.1.call-update) | async-done | bytes 1228816 | tf_op jit(solution)/shard_map/reduce_scatter | solution.py:306
  824.8 2.9 reshape.434
  827.7 131.1 %reduce-scatter.8.cloned.1.call-done = bf16[240,7680]{1,0:T(8,128)(2,1)} async-done(((bf16[960,7680]{1,0:T(8,128)(2,1)}), bf16[240,7680]{1,0:T(8,128)(2,1)}) %reduce-scatter.8.cloned.1.call-update) | async-done | bytes 3686416 | tf_op jit(solution)/shard_map/reduce_scatter | solution.py:33
  964.5 3.3 fusion.145
  970.7 3.7 reshape.433
  983.4 4.5 fusion.95
  994.0 69.2 %psum.14 = f32[1920]{0:T(1024)S(1)} all-reduce(f32[1920]{0:T(1024)S(1)} %pad_maximum_fusion.4), channel_id=1, replica_groups=mesh['ctx'=32,'fsdp'=4] {'ctx','fsdp'}, use_global_device_ids=true, to_apply=%region_15.16 | all-reduce | flops 1920 | bytes 15360 | tf_op jit(solution)/shard_map/psum | solution.py:39
  1065.5 266.6 %all-reduce.2.cloned.1.call-done = bf16[2457600]{0:T(1024)(128)(2,1)} async-done(((bf16[2457600]{0:T(1024)(128)(2,1)}), bf16[2457600]{0:T(1024)(128)(2,1)}) %all-reduce.2.cloned.1.call-update) | async-done | bytes 4915216 | tf_op jit(solution)/shard_map/psum | solution.py:39
  1339.0 4.7 slice_convert_fusion
  1343.7 3.4 reshape.442
  (286 shorter events, 104.6 us)
Async XLA Ops:
  7.2 151.5 %all-gather.5.cloned.1.call-start = ((), (), s32[]{:S(2)}) async-start(), calls=%async_computation.3 | async-start | bytes 18739200 | tf_op jit(solution)/shard_map/all_gather | solution.py:18
  10.9 8.5 copy-start.1
  18.6 144.4 %copy-start.39 = (s32[64]{0:T(128)S(1)}, s32[64]{0:T(128)}, u32[]{:S(2)}) copy-start(s32[64]{0:T(128)} %param.20) | copy-start | bytes 772
  18.6 195.2 %copy-start.13 = (bf16[1,128,960]{1,2,0:T(8,128)(2,1)S(1)}, bf16[1,128,960]{1,2,0:T(8,128)(2,1)}, u32[]{:S(2)}) copy-start(bf16[1,128,960]{1,2,0:T(8,128)(2,1)} %param.19) | copy-start | bytes 737284
  18.6 195.2 %all-gather.11.cloned.1.call-start = ((), (), s32[]{:S(2)}) async-start(), calls=%async_computation.6 | async-start | bytes 6144000 | tf_op jit(solution)/shard_map/all_gather | solution.py:124
  19.4 269.7 %all-gather.7.cloned.1.call-start = ((), (), s32[]{:S(2)}) async-start(), calls=%async_computation.4 | async-start | bytes 2703360 | tf_op jit(solution)/shard_map/all_gather | solution.py:150
  19.6 205.2 %copy-start.37 = (f32[128]{0:T(128)}, f32[128]{0:T(128)S(1)}, u32[]{:S(2)}) copy-start(f32[128]{0:T(128)S(1)} %add_rsqrt_fusion.1) | copy-start | bytes 1540
  160.1 64.8 %copy-start.34 = (f32[960]{0:T(1024)}, f32[960]{0:T(1024)S(1)}, u32[]{:S(2)}) copy-start(f32[960]{0:T(1024)S(1)} %get-tuple-element.357) | copy-start | bytes 11524
  163.0 200.8 %all-gather.9.cloned.1.call-start = ((), (), s32[]{:S(2)}) async-start(), calls=%async_computation.5 | async-start | bytes 2703360 | tf_op jit(solution)/shard_map/all_gather | solution.py:149
  164.1 61.6 %copy-start.24 = (f32[128,64]{0,1:T(8,128)}, f32[128,64]{0,1:T(8,128)S(1)}, u32[]{:S(2)}) copy-start(f32[128,64]{0,1:T(8,128)S(1)} %get-tuple-element.443) | copy-start | bytes 98308
  167.1 584.1 %reduce-scatter.10.cloned.1.call-start = ((), (), s32[]{:S(2)}) async-start(), calls=%async_computation.9 | async-start | bytes 5406720
  431.3 3.8 copy-start.22
  431.4 8.5 copy-start.21
  435.1 20.1 %copy-start.9 = (f32[128,960]{0,1:T(8,128)}, f32[128,960]{0,1:T(8,128)S(1)}, u32[]{:S(2)}) copy-start(f32[128,960]{0,1:T(8,128)S(1)} %get-tuple-element.451) | copy-start | bytes 1474564
  435.3 10.2 copy-start.3
  445.5 9.6 copy-start.26
  445.5 9.6 copy-start.28
  450.5 4.7 copy-start.14
  450.5 8.2 copy-start.20
  455.4 0.8 copy-start.6
  458.7 0.7 copy-start.32
  472.5 8.4 copy-start
  472.5 8.4 copy-start.18
  472.5 8.4 copy-start.33
  483.0 1.5 copy-start.19
  497.2 8.5 copy-start
  497.2 8.5 copy-start.18
  497.2 8.5 copy-start.33
  507.8 1.5 copy-start.19
  522.0 8.4 copy-start
  522.0 8.4 copy-start.18
  522.0 8.4 copy-start.33
  532.5 1.5 copy-start.19
  546.7 8.5 copy-start
  546.7 8.5 copy-start.18
  546.7 8.5 copy-start.33
  557.2 1.5 copy-start.19
  558.9 5.1 copy-start.5
  578.5 0.9 copy-start.15
  578.5 1.2 copy-start.16
  578.5 246.3 %reduce-scatter.12.cloned.1.call-start = ((), (), s32[]{:S(2)}) async-start(), calls=%async_computation.10 | async-start | bytes 6553600 | tf_op jit(solution)/shard_map/reduce_scatter | solution.py:306
  591.2 0.8 copy-start.31
  591.2 1.6 copy-start.36
  591.2 1.7 copy-start.2
  591.3 1.8 copy-start.35
  591.3 1.8 copy-start.38
  591.3 367.5 %reduce-scatter.8.cloned.1.call-start = ((), (), s32[]{:S(2)}) async-start(), calls=%async_computation.7 | async-start | bytes 18432000 | tf_op jit(solution)/shard_map/reduce_scatter | solution.py:33
  591.6 2.2 copy-start.7
  591.6 2.2 copy-start.23
  591.6 4.1 copy-start.4
  591.6 4.1 copy-start.29
  591.6 1.3 copy-start.11
  595.7 3.6 copy-start.27
  599.3 152.9 %copy-start.25 = (f32[128,64]{0,1:T(8,128)S(1)}, f32[128,64]{0,1:T(8,128)}, u32[]{:S(2)}) copy-start(f32[128,64]{0,1:T(8,128)} %copy-done.24) | copy-start | bytes 98308
  782.0 550.1 %all-reduce.2.cloned.1.call-start = ((), (), s32[]{:S(2)}) async-start(), calls=%async_computation.8 | async-start | bytes 9830400 | tf_op jit(solution)/shard_map/psum | solution.py:39
  978.6 3.7 copy-start.12
  981.0 2.4 copy-start.10
  981.0 2.4 copy-start.17
  982.2 7.4 copy-start.30
  987.9 76.6 %copy-start.8 = (f32[128,960]{0,1:T(8,128)S(1)}, f32[128,960]{0,1:T(8,128)}, u32[]{:S(2)}) copy-start(f32[128,960]{0,1:T(8,128)} %copy-done.6) | copy-start | bytes 1474564
Sparse Core Ops, SparseCore 0:
  18.7 139.9 all-gather.4
  160.4 53.3 all-gather.10
  217.2 71.8 all-gather.6
  292.2 71.5 all-gather.8
  578.6 172.4 reduce-scatter.9
  753.4 71.3 reduce-scatter.11
  827.2 131.4 reduce-scatter.7
  982.4 349.7 all-reduce.1
where the time goes:
time: 1390 us; the launch traced here: 1360 us
  waiting for transfers between devices  906 us (65%)
  matrix products  189 us (14%)
  local copies, waits for them, and re-layouts  138 us (10%)
  blocking collectives  69.2 us (5%)
  other arithmetic  41.4 us (3%)
  between operations  15.3 us (1%)
    psum x1, waiting for transfers between devices, together(): subtotal = lax.psum(ravelled, axis)  267 us
    unnamed x9, waiting for transfers between devices  149 us
    all_gather x1, waiting for transfers between devices, sent_together(): result, at, done = (lax.all_gather(both, axis, axis=dim, tiled=True), 0, [])  139 us
    reduce_scatter x1, waiting for transfers between devices, sent_together_2(): lax.psum_scatter(both, axis, scatter_dimension=dim, tiled=True)  131 us
    psum x1, blocking collectives, together(): subtotal = lax.psum(ravelled, axis)  69.2 us
    all_gather x1, waiting for transfers between devices, on_device(): lax.all_gather(keys_low, 'ctx', axis=0, tiled=True)  68.1 us
    all_gather x1, waiting for transfers between devices, on_device(): lax.all_gather(value_low, 'ctx', axis=0, tiled=True)  63.3 us
    all_gather x1, waiting for transfers between devices, on_device(): lax.all_gather(w_down, 'fsdp', axis=0, tiled=True)  46.1 us
  transfers between devices with their start and end apart: 8, of which 8 were waited for; matrix products, arithmetic and copies ran while one was open for 7% of the time, Pallas kernels for 0%

commit v1 on v0

v1 whole, which is shorter than its diff:
```python
import functools
import math

import jax
import jax.numpy as jnp
from jax import lax
from jax.experimental import pallas as pl
from jax.experimental.pallas import tpu as pltpu
from jax.sharding import PartitionSpec as P

D = 960
HEADS = 15
KV_HEADS = 5
GROUP = 3
HEAD = 64
FF = 2560
TOK = 128
HALF = 64
CTX = 32
TILES = 33
KEYS = TILES * 128
SCALE = HEAD ** (-0.5)
EPSILON = 1e-05
BASE = 10000.0
LOG2E = math.log2(math.e)
NEG = -1e30
MESH = pl.DeviceIdType.MESH
ANY = pl.BlockSpec(memory_space=pl.ANY)
VM = pl.BlockSpec(memory_space=pltpu.VMEM)
BIG = 56 * 2**20
F32 = jnp.float32
BF16 = jnp.bfloat16


def here():
    ctx = lax.axis_index("ctx")
    shard = lax.axis_index("fsdp")
    return {
        "z": ctx // 8,
        "yh": (ctx // 4) % 2,
        "x": ctx % 4,
        "yl": shard // 2,
        "c": shard % 2,
    }


def device(place, **moved):
    p = {**place, **moved}
    return (p["z"] * 8 + p["yh"] * 4 + p["x"], p["yl"] * 2 + p["c"])


def greet(devices):
    sem = pltpu.get_barrier_semaphore()
    for d in devices:
        pl.semaphore_signal(sem, inc=1, device_id=d, device_id_type=MESH)
    pl.semaphore_wait(sem, len(devices))


class Sems:
    def __init__(self, send, recv):
        self.send, self.recv, self.at = send, recv, 0

    def push(self, src, dst, dev):
        copy = pltpu.make_async_remote_copy(
            src_ref=src,
            dst_ref=dst,
            send_sem=self.send.at[self.at],
            recv_sem=self.recv.at[self.at],
            device_id=dev,
            device_id_type=MESH,
        )
        self.at += 1
        copy.start()
        return copy


def gather_kernel(count, *refs):
    ins, outs = refs[:count], refs[count : 2 * count]
    send, recv, local = refs[2 * count :]
    me = here()
    f = me["yl"] * 2 + me["c"]
    near = device(me, yl=1 - me["yl"])
    far = device(me, yl=1 - me["yl"], yh=1 - me["yh"])
    mate = device(me, c=1 - me["c"])
    across = (1 - me["yl"]) * 2 + me["c"]
    greet((near, far, mate))
    sems = Sems(send, recv)
    parts, kept, own = [], [], []
    for i, (a, b) in enumerate(zip(ins, outs)):
        rows = a.shape[0]
        first = rows // 32 * 16 if i % 2 else (rows + 31) // 32 * 16
        first = max(first, 0)
        spans = [(0, first, near), (first, rows - first, far)]
        for lo, size, dev in spans:
            if size:
                src = a.at[pl.ds(lo, size)]
                dst = b.at[pl.ds(pl.multiple_of(f * rows + lo, 16), size)]
                parts.append((sems.push(src, dst, dev), b, rows, lo, size))
    for i, (a, b) in enumerate(zip(ins, outs)):
        rows = a.shape[0]
        dst = b.at[pl.ds(pl.multiple_of(f * rows, 16), rows)]
        kept.append(sems.push(a, dst, mate))
        copy = pltpu.make_async_copy(a, dst, local.at[i])
        copy.start()
        own.append(copy)
    for copy, b, rows, lo, size in parts:
        copy.wait_recv()
        span = b.at[pl.ds(pl.multiple_of(across * rows + lo, 16), size)]
        kept.append(sems.push(span, span, mate))
    for copy in own:
        copy.wait()
    for copy in kept:
        copy.wait()
    for copy, *_ in parts:
        copy.wait_send()


def gather_weights(arrays, collective_id):
    n = len(arrays)
    copies = 5 * n
    return pl.pallas_call(
        functools.partial(gather_kernel, n),
        out_shape=[jax.ShapeDtypeStruct((4 * a.shape[0], *a.shape[1:]), a.dtype) for a in arrays],
        in_specs=[ANY] * n,
        out_specs=[ANY] * n,
        scratch_shapes=[
            pltpu.SemaphoreType.DMA((copies,)),
            pltpu.SemaphoreType.DMA((copies,)),
            pltpu.SemaphoreType.DMA((n,)),
        ],
        compiler_params=pltpu.CompilerParams(collective_id=collective_id, has_side_effects=True),
        name="gather_weights",
    )(*arrays)


def around(me, axis):
    return [(d, lax.rem(me[axis] + d, 4)) for d in (1, 3, 2)]


def kv_gather_kernel(kv, out, send, recv, local):
    me = here()
    x, yh, z = me["x"], me["yh"], me["z"]
    other = device(me, yh=1 - yh)
    xs = [(at, device(me, x=at)) for _, at in around(me, "x")]
    zs = [(at, device(me, z=at)) for _, at in around(me, "z")]
    greet([other] + [d for _, d in xs] + [d for _, d in zs])
    sems = Sems(send, recv)
    key, value = pl.ds(0, 320), pl.ds(320, 320)
    mine = pltpu.make_async_copy(kv, out.at[z, yh, x], local.at[0])
    mine.start()
    done = []
    step1 = [sems.push(kv.at[p], out.at[z, yh, x, p], other) for p in (key, value)]
    step2 = {(0, 0): [], (0, 1): [], (1, 0): [], (1, 1): []}
    for _, dev in xs:
        step2[0, 0].append(sems.push(kv.at[key], out.at[z, yh, x, key], dev))
    for _, dev in zs:
        step2[1, 0].append(sems.push(kv.at[value], out.at[z, yh, x, value], dev))
    for axis, (devs, p) in enumerate(((xs, key), (zs, value))):
        step1[axis].wait_recv()
        span = out.at[z, 1 - yh, x, p]
        for _, dev in devs:
            step2[axis, 1].append(sems.push(span, span, dev))
    mine.wait()
    step3 = []
    for hop in (0, 1):
        row = yh if hop == 0 else 1 - yh
        for c in step2[0, hop]:
            c.wait_recv()
        span = out.at[z, row, :, key]
        for _, dev in zs:
            step3.append(sems.push(span, span, dev))
        for c in step2[1, hop]:
            c.wait_recv()
        span = out.at[:, row, x, value]
        for _, dev in xs:
            step3.append(sems.push(span, span, dev))
    for c in step3:
        c.wait_recv()
    for c in step1 + sum(step2.values(), []) + step3:
        c.wait_send()


def gather_kv(kv, collective_id):
    return pl.pallas_call(
        kv_gather_kernel,
        out_shape=jax.ShapeDtypeStruct((4, 2, 4, 640, 128), BF16),
        in_specs=[ANY],
        out_specs=ANY,
        scratch_shapes=[
            pltpu.SemaphoreType.DMA((26,)),
            pltpu.SemaphoreType.DMA((26,)),
            pltpu.SemaphoreType.DMA((1,)),
        ],
        compiler_params=pltpu.CompilerParams(collective_id=collective_id, has_side_effects=True),
        name="gather_kv",
    )(kv).reshape(CTX, 640, 128)


def kv_scatter_kernel(part, out, r1a, r1b, s1a, s1b, r2a, r2b, s2, r3, send, recv):
    me = here()
    x, yh, z = me["x"], me["yh"], me["z"]
    other = device(me, yh=1 - yh)
    xs = [(d, at, device(me, x=at)) for d, at in around(me, "x")]
    zs = [(d, at, device(me, z=at)) for d, at in around(me, "z")]
    greet([other] + [d for *_, d in xs] + [d for *_, d in zs])
    sems = Sems(send, recv)
    key, value = pl.ds(0, 320), pl.ds(320, 320)
    rows = (1 - yh, yh)
    first = {}
    for row in (0, 1):
        for d, at, dev in zs:
            first[0, row, d] = sems.push(part.at[at, rows[row], :, key], r1a.at[d - 1, row], dev)
        for d, at, dev in xs:
            first[1, row, d] = sems.push(part.at[:, rows[row], at, value], r1b.at[d - 1, row], dev)
    second = {}
    for row in (0, 1):
        for axis, (r1, s1) in enumerate(((r1a, s1a), (r1b, s1b))):
            for d in (1, 2, 3):
                first[axis, row, d].wait_recv()
            for i in range(4):
                own = part[z, rows[row], i, 0:320] if axis == 0 else part[i, rows[row], x, 320:640]
                total = own.astype(F32)
                for d in (0, 1, 2):
                    total = total + r1[d, row, i].astype(F32)
                s1[row, i] = total.astype(BF16)
            ring, r2 = ((xs, r2a), (zs, r2b))[axis]
            for d, at, dev in ring:
                second[axis, row, d] = sems.push(s1.at[row, at], r2.at[d - 1, row], dev)
    third = []
    for row in (0, 1):
        for axis, (s1, r2) in enumerate(((s1a, r2a), (s1b, r2b))):
            at = x if axis == 0 else z
            for d in (1, 2, 3):
                second[axis, row, d].wait_recv()
            total = s1[row, at].astype(F32)
            for d in (0, 1, 2):
                total = total + r2[d, row].astype(F32)
            if row == 0:
                s2[axis] = total.astype(BF16)
                third.append(sems.push(s2.at[axis], r3.at[axis], other))
            else:
                out[pl.ds(axis * 320, 320), :] = total
    for axis in (0, 1):
        third[axis].wait_recv()
        span = pl.ds(axis * 320, 320)
        out[span, :] = out[span, :] + r3[axis].astype(F32)
    for c in list(first.values()) + list(second.values()) + third:
        c.wait_send()


def scatter_kv(part, collective_id):
    return pl.pallas_call(
        kv_scatter_kernel,
        out_shape=jax.ShapeDtypeStruct((640, 128), F32),
        in_specs=[VM],
        out_specs=VM,
        scratch_shapes=[
            pltpu.VMEM((3, 2, 4, 320, 128), BF16),
            pltpu.VMEM((3, 2, 4, 320, 128), BF16),
            pltpu.VMEM((2, 4, 320, 128), BF16),
            pltpu.VMEM((2, 4, 320, 128), BF16),
            pltpu.VMEM((3, 2, 320, 128), BF16),
            pltpu.VMEM((3, 2, 320, 128), BF16),
            pltpu.VMEM((2, 320, 128), BF16),
            pltpu.VMEM((2, 320, 128), BF16),
            pltpu.SemaphoreType.DMA((26,)),
            pltpu.SemaphoreType.DMA((26,)),
        ],
        compiler_params=pltpu.CompilerParams(
            collective_id=collective_id, has_side_effects=True, vmem_limit_bytes=BIG
        ),
        name="scatter_kv",
    )(part.reshape(4, 2, 4, 640, 128))


def tile_plan(block_table, ctx):
    early = jnp.min(block_table.reshape(CTX, 2), axis=1)
    mine = lax.dynamic_index_in_dim(early, ctx, keepdims=False)
    late_turn = (early >= mine)[:, None]
    offset = jnp.arange(HALF, dtype=jnp.int32)[None, :]
    m = jnp.broadcast_to(late_turn.astype(F32), (CTX, HALF))
    one, zero = jnp.ones_like(m), jnp.zeros_like(m)

    def rows(a, b, last):
        return jnp.concatenate([jnp.concatenate([a, b], axis=1), last], axis=0)

    blank = jnp.zeros((1, 128), F32)
    flags = rows(one, m, blank)
    left = rows(m, 1.0 - m, blank)
    right = rows(1.0 - m, zero, blank)
    t_first = (early[:, None] - (63 - mine)) * HALF + offset
    t_second = jnp.where(late_turn, mine - early[:, None], early[:, None] - mine) * HALF + offset
    t_last = jnp.concatenate([offset, jnp.full((1, HALF), 10**6, jnp.int32)], axis=1)
    limits = rows(t_first.astype(F32), t_second.astype(F32), t_last.astype(F32))
    return flags, left, right, limits


def build_tiles(head, kv_ref, own_ref, left_ref, tiles_ref, base):
    lane = lax.broadcasted_iota(jnp.int32, (HALF, 128), 1)
    start = pl.multiple_of(base + head * HALF, HALF)

    def one(i, _):
        block = kv_ref[i, pl.ds(start, HALF), :].astype(F32)
        top = jnp.where(lane < HALF, block, 0.0)
        low = pltpu.roll(block, HALF, 1) * left_ref[pl.ds(i, 1), :]
        at = pl.multiple_of(i * 128, 128)
        tiles_ref[pl.ds(at, 128), :] = jnp.concatenate([top, low], axis=0).astype(BF16)
        return 0

    lax.fori_loop(0, CTX, one, 0, unroll=4)
    block = own_ref[pl.ds(start, HALF), :].astype(F32)
    top = jnp.where(lane < HALF, 0.0, pltpu.roll(block, HALF, 1))
    tiles_ref[pl.ds(CTX * 128, 128), :] = jnp.concatenate(
        [top, jnp.zeros_like(top)], axis=0
    ).astype(BF16)


def dot_nt(a, b):
    return lax.dot_general(a, b, (((1,), (1,)), ((), ())), preferred_element_type=F32)


def dot_nn(a, b):
    return lax.dot_general(a, b, (((1,), (0,)), ((), ())), preferred_element_type=F32)


ROWS = GROUP * HALF
STEP = 3


def row_offset():
    return lax.rem(lax.broadcasted_iota(jnp.int32, (ROWS, 128), 0), HALF).astype(F32)


def attend_kernel(q_ref, kv_ref, own_ref, flag_ref, left_ref, limit_ref, o_ref, l_ref, kk, vv, s_ref):
    head = pl.program_id(0)
    build_tiles(head, kv_ref, own_ref, left_ref, kk, 0)
    build_tiles(head, kv_ref, own_ref, left_ref, vv, 320)
    q = q_ref[0]
    offset = row_offset()
    low = jnp.full((ROWS, 128), NEG, F32)

    def scores(j, carry):
        top_l, top_e = carry
        at = pl.multiple_of(j * STEP * 128, 128)
        s = dot_nt(q, kk[pl.ds(at, STEP * 128), :]) * (SCALE * LOG2E)
        for t in range(STEP):
            i = j * STEP + t
            tile = s[:, t * 128 : (t + 1) * 128]
            tile = jnp.where(limit_ref[pl.ds(i, 1), :] <= offset, tile, NEG)
            late = flag_ref[pl.ds(i, 1), :] > 0.5
            top_l = jnp.maximum(top_l, jnp.where(late, tile, NEG))
            top_e = jnp.maximum(top_e, jnp.where(late, NEG, tile))
            s_ref[:, pl.ds(pl.multiple_of(at + t * 128, 128), 128)] = tile
        return top_l, top_e

    top_l, top_e = lax.fori_loop(0, TILES // STEP, scores, (low, low))
    max_l = jnp.broadcast_to(jnp.max(top_l, axis=1, keepdims=True), (ROWS, 128))
    max_e = jnp.broadcast_to(jnp.max(top_e, axis=1, keepdims=True), (ROWS, 128))
    zero = jnp.zeros((ROWS, 128), F32)

    def values(j, carry):
        sum_l, sum_e, total = carry
        at = pl.multiple_of(j * STEP * 128, 128)
        probs = []
        for t in range(STEP):
            i = j * STEP + t
            tile = s_ref[:, pl.ds(pl.multiple_of(at + t * 128, 128), 128)]
            late = flag_ref[pl.ds(i, 1), :] > 0.5
            p = jnp.exp2(tile - jnp.where(late, max_l, max_e))
            p_l = jnp.where(late, p, 0.0)
            sum_l = sum_l + p_l
            sum_e = sum_e + (p - p_l)
            probs.append(p.astype(BF16))
        total = total + dot_nn(jnp.concatenate(probs, axis=1), vv[pl.ds(at, STEP * 128), :])
        return sum_l, sum_e, total

    sum_l, sum_e, total = lax.fori_loop(0, TILES // STEP, values, (zero, zero, zero))
    late = lax.broadcasted_iota(jnp.int32, (ROWS, 128), 1) < HALF
    row_sum = jnp.where(
        late, jnp.sum(sum_l, axis=1, keepdims=True), jnp.sum(sum_e, axis=1, keepdims=True)
    )
    o_ref[0] = total / row_sum
    l_ref[0] = jnp.where(late, max_l, max_e) + jnp.log2(row_sum)


def head_spec(*shape):
    return pl.BlockSpec((1, *shape), lambda h: (h, 0, 0))


def whole_spec(*shape):
    return pl.BlockSpec(shape, lambda h: (0,) * len(shape))


def attend(q, kv, own, plan):
    flags, left, _, limits = plan
    return pl.pallas_call(
        attend_kernel,
        grid=(KV_HEADS,),
        out_shape=[jax.ShapeDtypeStruct((KV_HEADS, ROWS, 128), F32)] * 2,
        in_specs=[
            head_spec(ROWS, 128),
            whole_spec(CTX, 640, 128),
            whole_spec(640, 128),
            whole_spec(TILES, 128),
            whole_spec(TILES, 128),
            whole_spec(TILES, 128),
        ],
        out_specs=[head_spec(ROWS, 128)] * 2,
        scratch_shapes=[
            pltpu.VMEM((KEYS, 128), BF16),
            pltpu.VMEM((KEYS, 128), BF16),
            pltpu.VMEM((ROWS, KEYS), F32),
        ],
        compiler_params=pltpu.CompilerParams(vmem_limit_bytes=BIG),
        name="attend",
    )(q, kv, own, flags, left, limits)


def attend_back_kernel(
    q_ref, qt_ref, do_ref, dot_ref, o_ref, l_ref, kv_ref, own_ref, flag_ref, left_ref, right_ref,
    limit_ref, dq_ref, dkv_ref, kk, vv,
):
    head = pl.program_id(0)
    build_tiles(head, kv_ref, own_ref, left_ref, kk, 0)
    build_tiles(head, kv_ref, own_ref, left_ref, vv, 320)
    q, qt, do, dot = q_ref[0], qt_ref[0], do_ref[0], dot_ref[0]
    offset = row_offset()
    lane = lax.broadcasted_iota(jnp.int32, (ROWS, 128), 1)
    product = do.astype(F32) * o_ref[0]
    shape = (ROWS, 128)
    delta_l = jnp.broadcast_to(
        jnp.sum(jnp.where(lane < HALF, product, 0.0), axis=1, keepdims=True), shape
    )
    delta_e = jnp.broadcast_to(
        jnp.sum(jnp.where(lane < HALF, 0.0, product), axis=1, keepdims=True), shape
    )
    log_l = jnp.broadcast_to(l_ref[0][:, 0:1], shape)
    log_e = jnp.broadcast_to(l_ref[0][:, HALF : HALF + 1], shape)
    k_rows = pl.ds(pl.multiple_of(head * HALF, HALF), HALF)
    v_rows = pl.ds(pl.multiple_of(320 + head * HALF, HALF), HALF)
    small = lax.broadcasted_iota(jnp.int32, (HALF, 128), 1)

    def grads(j, total):
        at = pl.multiple_of(j * STEP * 128, 128)
        keys = kk[pl.ds(at, STEP * 128), :]
        s = dot_nt(q, keys) * (SCALE * LOG2E)
        dp = dot_nt(do, vv[pl.ds(at, STEP * 128), :])
        probs, scores = [], []
        for t in range(STEP):
            i = j * STEP + t
            cut = slice(t * 128, (t + 1) * 128)
            late = flag_ref[pl.ds(i, 1), :] > 0.5
            tile = jnp.where(limit_ref[pl.ds(i, 1), :] <= offset, s[:, cut], NEG)
            p = jnp.exp2(tile - jnp.where(late, log_l, log_e))
            probs.append(p.astype(BF16))
            scores.append((p * (dp[:, cut] - jnp.where(late, delta_l, delta_e))).astype(BF16))
        ds = jnp.concatenate(scores, axis=1)
        total = total + dot_nn(ds, keys)
        dk = dot_nn(qt, ds) * SCALE
        dv = dot_nn(dot, jnp.concatenate(probs, axis=1))
        for t in range(STEP):
            i = j * STEP + t
            cut = slice(t * 128, (t + 1) * 128)
            for rows, both in ((k_rows, dk), (v_rows, dv)):
                top, bottom = both[0:HALF, cut], both[HALF:128, cut]

                @pl.when(i < CTX)
                def _():
                    dkv_ref[i, rows, :] = (
                        top * flag_ref[pl.ds(i, 1), :]
                        + pltpu.roll(bottom, HALF, 1) * right_ref[pl.ds(i, 1), :]
                    ).astype(BF16)

                @pl.when(i == CTX)
                def _():
                    mine = lax.axis_index("ctx")
                    before = dkv_ref[mine, rows, :].astype(F32)
                    dkv_ref[mine, rows, :] = (
                        before + jnp.where(small < HALF, bottom, 0.0)
                    ).astype(BF16)

        return total

    total = lax.fori_loop(0, TILES // STEP, grads, jnp.zeros(shape, F32))
    dq_ref[0] = total * SCALE


def attend_back(q, do, o, logs, kv, own, plan):
    flags, left, right, limits = plan
    return pl.pallas_call(
        attend_back_kernel,
        grid=(KV_HEADS,),
        out_shape=[
            jax.ShapeDtypeStruct((KV_HEADS, ROWS, 128), F32),
            jax.ShapeDtypeStruct((CTX, 640, 128), BF16),
        ],
        in_specs=[
            head_spec(ROWS, 128),
            head_spec(128, ROWS),
            head_spec(ROWS, 128),
            head_spec(128, ROWS),
            head_spec(ROWS, 128),
            head_spec(ROWS, 128),
            whole_spec(CTX, 640, 128),
            whole_spec(640, 128),
            whole_spec(TILES, 128),
            whole_spec(TILES, 128),
            whole_spec(TILES, 128),
            whole_spec(TILES, 128),
        ],
        out_specs=[head_spec(ROWS, 128), whole_spec(CTX, 640, 128)],
        scratch_shapes=[pltpu.VMEM((KEYS, 128), BF16), pltpu.VMEM((KEYS, 128), BF16)],
        compiler_params=pltpu.CompilerParams(vmem_limit_bytes=BIG),
        name="attend_back",
    )(
        q, jnp.swapaxes(q, 1, 2), do, jnp.swapaxes(do, 1, 2), o, logs, kv, own,
        flags, left, right, limits,
    )


def to_rows(a):
    a = a.reshape(2, HALF, KV_HEADS, GROUP, HEAD)[::-1]
    return a.transpose(2, 3, 1, 0, 4).reshape(KV_HEADS, ROWS, 128)


def from_rows(a):
    a = a.reshape(KV_HEADS, GROUP, HALF, 2, HEAD).transpose(3, 2, 0, 1, 4)[::-1]
    return a.reshape(TOK, HEADS * HEAD)


def to_wire(a):
    return a.reshape(2, HALF, KV_HEADS, HEAD).transpose(2, 1, 0, 3).reshape(KV_HEADS * HALF, 128)


def reduce_kernel(jobs, used, pa, pb, extra, *refs):
    refs = list(refs)
    sources = []
    for shared_left, _, shared_right, _ in jobs:
        left = [refs.pop(0) for _ in range(1 if shared_left else 2)]
        right = [refs.pop(0) for _ in range(1 if shared_right else 2)]
        sources.append((left[0], left[-1], right[0], right[-1]))
    if extra:
        extra_refs = (refs.pop(0), refs.pop(0))
    out = refs.pop(0)
    buffers = [(refs.pop(0), refs.pop(0)) for _ in jobs]
    if extra:
        extra_buffer = refs.pop(0)
    grads = refs.pop(0)
    parts = [[refs.pop(0) for _ in range(6)] for _ in range(2)]
    send, recv, local = refs

    me = here()
    x, yh, z, yl = me["x"], me["yh"], me["z"], me["yl"]
    mate = device(me, c=1 - me["c"])
    xs = [(d, at, device(me, x=at)) for d, at in around(me, "x")]
    zs = [(d, at, device(me, z=at)) for d, at in around(me, "z")]
    near = device(me, yl=1 - yl)
    far = device(me, yl=1 - yl, yh=1 - yh)
    same = device(me, yh=1 - yh)
    greet([mate, near, far, same] + [d for *_, d in xs] + [d for *_, d in zs])
    sems = Sems(send, recv)

    mine, traded = [], []
    for (lm, lt, rm, rt), (lb, rb) in zip(sources, buffers):
        traded.append(sems.push(lt, lb.at[:, :, pl.ds(128, 128)], mate))
        traded.append(sems.push(rt, rb.at[:, pl.ds(128, 128)], mate))
        for src, dst in ((lm, lb.at[:, :, pl.ds(0, 128)]), (rm, rb.at[:, pl.ds(0, 128)])):
            copy = pltpu.make_async_copy(src, dst, local.at[len(mine)])
            copy.start()
            mine.append(copy)
    if extra:
        traded.append(sems.push(extra_refs[1], extra_buffer.at[1], mate))
        copy = pltpu.make_async_copy(extra_refs[0], extra_buffer.at[0], local.at[len(mine)])
        copy.start()
        mine.append(copy)
    for copy in mine:
        copy.wait()
    for copy in traded:
        copy.wait_recv()

    base = 0
    for (_, m, _, n), (lb, rb) in zip(jobs, buffers):
        width = 256 if n % 256 == 0 else 128
        for s in range(2):
            left = lb[min(s, lb.shape[0] - 1)]

            def block(i, _, left=left, rb=rb, s=s, m=m, width=width, base=base):
                at = pl.multiple_of(i * width, 128)
                right = rb[min(s, rb.shape[0] - 1), :, pl.ds(at, width)]
                result = dot_nn(left, right).astype(BF16)
                for w in range(width // 128):
                    to = pl.multiple_of(base + (i * (width // 128) + w) * m, 16)
                    grads[s, pl.ds(to, m), :] = result[:, w * 128 : (w + 1) * 128]
                return 0

            lax.fori_loop(0, n // width, block, 0)
        base += m * (n // 128)
    if extra:
        for s in range(2):
            both = extra_buffer[0, s].astype(F32) + extra_buffer[1, s].astype(F32)
            grads[s, pl.ds(base, 16), :] = both.astype(BF16)
        base += 16
    if base < used:
        for s in range(2):
            grads[s, pl.ds(base, used - base), :] = jnp.zeros((used - base, 128), BF16)

    plans = (
        (0, pa, xs, zs, x, z, parts[0]),
        (16 * pa, pb, zs, xs, z, x, parts[1]),
    )
    order = (1, 3, 2, 0)
    first, second = {}, {}
    sent = []
    for k in order:
        for n, (lo, size, ring, cross, i_me, j_me, _) in enumerate(plans):
            r1 = parts[n][0]
            j = lax.rem(j_me + k, 4)
            for d, at, dev in ring:
                src = grads.at[:, pl.ds(pl.multiple_of(lo + (at * 4 + j) * size, 16), size)]
                first[n, k, d] = sems.push(src, r1.at[d - 1, k], dev)
    for k in order:
        for n, (lo, size, ring, cross, i_me, j_me, (r1, s1, r2, s2, r3, fin)) in enumerate(plans):
            j = lax.rem(j_me + k, 4)
            for d in (1, 2, 3):
                first[n, k, d].wait_recv()
            for s in range(2):
                own = grads[s, pl.ds(pl.multiple_of(lo + (i_me * 4 + j) * size, 16), size)]
                total = own.astype(F32)
                for d in (0, 1, 2):
                    total = total + r1[d, k, s].astype(F32)
                s1[k, s] = total.astype(BF16)
            if k:
                dev = [dev for d, _, dev in cross if d == k][0]
                second[n, k] = sems.push(s1.at[k], r2.at[k - 1], dev)
    third = {}
    for n, (lo, size, ring, cross, i_me, j_me, (r1, s1, r2, s2, r3, fin)) in enumerate(plans):
        for k in (1, 2, 3):
            second[n, k].wait_recv()
        for s in range(2):
            total = s1[0, s].astype(F32)
            for d in (0, 1, 2):
                total = total + r2[d, s].astype(F32)
            s2[s] = total.astype(BF16)
        slot = r3.at[yl * 2 + yh]
        third[n, 0] = sems.push(s2.at[1 - yl], slot, near)
        third[n, 1] = sems.push(s2.at[1 - yl], slot, far)
        third[n, 2] = sems.push(s2.at[yl], slot, same)
    fourth, fifth = {}, {}
    for n, (lo, size, ring, cross, i_me, j_me, (r1, s1, r2, s2, r3, fin)) in enumerate(plans):
        r3[yl * 2 + yh] = s2[yl]
        for i in (0, 1, 2):
            third[n, i].wait_recv()
        total = r3[0].astype(F32)
        for i in (1, 2, 3):
            total = total + r3[i].astype(F32)
        fin[...] = total.astype(BF16)
        span = out.at[pl.ds(pl.multiple_of(lo + (i_me * 4 + j_me) * size, 16), size)]
        copy = pltpu.make_async_copy(fin, span, local.at[n])
        copy.start()
        fourth[n, "own"] = copy
        for d, _, dev in cross:
            fourth[n, d] = sems.push(fin, span, dev)
        for d, _, dev in ring:
            fifth[n, 0, d] = sems.push(fin, span, dev)
    for back in (3, 1, 2):
        for n, (lo, size, ring, cross, i_me, j_me, _) in enumerate(plans):
            fourth[n, back].wait_recv()
            j = lax.rem(j_me + 4 - back, 4)
            span = out.at[pl.ds(pl.multiple_of(lo + (i_me * 4 + j) * size, 16), size)]
            for d, _, dev in ring:
                fifth[n, back, d] = sems.push(span, span, dev)
    for copy in fifth.values():
        copy.wait_recv()
    for n in (0, 1):
        fourth.pop((n, "own")).wait()
    for group in (traded, first.values(), second.values(), third.values()):
        for copy in group:
            copy.wait_send()
    for group in (fourth.values(), fifth.values()):
        for copy in group:
            copy.wait_send()


def reduce_grads(jobs, extra, collective_id):
    operands, shapes, buffers, rows = [], [], [], 0
    for left, right in jobs:
        shared_left, shared_right = not isinstance(left, tuple), not isinstance(right, tuple)
        lefts = [left] if shared_left else list(left)
        rights = [right] if shared_right else list(right)
        operands += lefts + rights
        m, n = lefts[0].shape[1], rights[0].shape[2]
        shapes.append((shared_left, m, shared_right, n))
        buffers.append(pltpu.VMEM((lefts[0].shape[0], m, 256), BF16))
        buffers.append(pltpu.VMEM((rights[0].shape[0], 256, n), BF16))
        rows += m * (n // 128)
    if extra is not None:
        operands += list(extra)
        buffers.append(pltpu.VMEM((2, 2, 16, 128), BF16))
        rows += 16
    pieces = -(-rows // 256)
    pa, pb = (pieces + 1) // 2 * 16, pieces // 2 * 16
    used = 16 * (pa + pb)
    scratch = buffers + [pltpu.VMEM((2, used, 128), BF16)]
    for size in (pa, pb):
        scratch += [
            pltpu.VMEM((3, 4, 2, size, 128), BF16),
            pltpu.VMEM((4, 2, size, 128), BF16),
            pltpu.VMEM((3, 2, size, 128), BF16),
            pltpu.VMEM((2, size, 128), BF16),
            pltpu.VMEM((4, size, 128), BF16),
            pltpu.VMEM((size, 128), BF16),
        ]
    copies = 2 * len(jobs) + 1 + 24 + 6 + 6 + 6 + 24
    scratch += [
        pltpu.SemaphoreType.DMA((copies,)),
        pltpu.SemaphoreType.DMA((copies,)),
        pltpu.SemaphoreType.DMA((2 * len(jobs) + 1,)),
    ]
    return pl.pallas_call(
        functools.partial(reduce_kernel, tuple(shapes), used, pa, pb, extra is not None),
        out_shape=jax.ShapeDtypeStruct((used, 128), BF16),
        in_specs=[ANY] * len(operands),
        out_specs=ANY,
        scratch_shapes=scratch,
        compiler_params=pltpu.CompilerParams(
            collective_id=collective_id, has_side_effects=True, vmem_limit_bytes=BIG
        ),
        name="reduce_grads",
    )(*operands)


def pick(a, axis, core):
    return lax.dynamic_index_in_dim(a, core, axis, keepdims=False)


def left_shards(a, core):
    t = a.T.reshape(2, 2, 240, TOK)
    return pick(t, 1, core), pick(t, 1, 1 - core)


def right_shards(a, core):
    t = a.reshape(TOK, 2, 2, a.shape[1] // 4).transpose(1, 2, 0, 3)
    return pick(t, 1, core), pick(t, 1, 1 - core)


def pad_lanes(a):
    extra = -a.shape[1] % 128
    return jnp.pad(a, ((0, 0), (0, extra)))


def unblock(flat, m, columns):
    blocks = -(-columns // 128)
    a = flat[: m * blocks].reshape(blocks, m, 128).transpose(1, 0, 2).reshape(m, blocks * 128)
    return a[:, :columns].astype(F32), flat[m * blocks :]


def norm_forward(values, gain):
    inv_rms = lax.rsqrt(jnp.mean(values * values, axis=-1, keepdims=True) + EPSILON)
    return values * inv_rms * gain, inv_rms


def norm_backward(values, inv_rms, gain, grad_normed):
    scaled = grad_normed * gain
    grad_values = inv_rms * scaled - values * inv_rms * inv_rms * inv_rms * jnp.mean(
        scaled * values, axis=-1, keepdims=True
    )
    grad_gain = jnp.sum(grad_normed * values * inv_rms, axis=0)
    return grad_values, grad_gain


def rope_tables(positions, half_dim):
    frequency = BASE ** (-jnp.arange(half_dim, dtype=F32) / half_dim)
    angles = positions.astype(F32)[:, None] * frequency[None, :]
    cosine = jnp.concatenate([jnp.cos(angles), jnp.cos(angles)], axis=-1)[:, None, :]
    sine = jnp.concatenate([jnp.sin(angles), jnp.sin(angles)], axis=-1)[:, None, :]
    return cosine, sine


def rotate(values, cosine, sine):
    half_dim = values.shape[-1] // 2
    turned = jnp.concatenate([-values[..., half_dim:], values[..., :half_dim]], axis=-1)
    return values * cosine + turned * sine


def dot(a, b):
    return jnp.dot(a, b, preferred_element_type=F32)


def swap_rows(a, swap):
    return jnp.where(swap, jnp.concatenate([a[HALF:], a[:HALF]], axis=0), a)


def on_device(
    tokens, cotangent, block_table, attn_gain, w_query, w_key, w_value, w_out, mlp_gain,
    w_gate, w_up, w_down,
):
    ctx = lax.axis_index("ctx")
    core = lax.axis_index("fsdp") % 2
    gains = jnp.pad(jnp.stack([attn_gain, mlp_gain]), ((0, 14), (0, 16)))
    qkv_shard = jnp.concatenate([w_query, w_key, w_value], axis=1)
    gains_all, qkv_w, out_w, gate_w, up_w, down_w = gather_weights(
        (gains, qkv_shard, w_out, w_gate, w_up, w_down), 0
    )
    gains_all = gains_all.reshape(4, 16, 256)[:, :2, :240].astype(F32)
    gain_a = gains_all[:, 0].reshape(D)
    gain_b = gains_all[:, 1].reshape(D)

    own_blocks = lax.dynamic_slice_in_dim(block_table, 2 * ctx, 2)
    swap = own_blocks[0] > own_blocks[1]
    early = jnp.min(own_blocks)
    offsets = jnp.arange(HALF, dtype=jnp.int32)
    positions = jnp.concatenate([early * HALF + offsets, (63 - early) * HALF + offsets])
    cosine, sine = rope_tables(positions, HEAD // 2)
    plan = tile_plan(block_table, ctx)

    resid_in = swap_rows(tokens[0], swap).astype(F32)
    grad_low = swap_rows(cotangent[0], swap)
    normed_a, inv_a = norm_forward(resid_in, gain_a)
    normed_a_low = normed_a.astype(BF16)
    qkv = dot(normed_a_low, qkv_w)
    value_low = qkv[:, 1280:].astype(BF16)
    queries = rotate(qkv[:, :960].reshape(TOK, HEADS, HEAD), cosine, sine).astype(BF16)
    keys = rotate(qkv[:, 960:1280].reshape(TOK, KV_HEADS, HEAD), cosine, sine).astype(BF16)
    q_rows = to_rows(queries)
    own_kv = jnp.concatenate([to_wire(keys), to_wire(value_low)], axis=0)
    kv = gather_kv(own_kv, 1)
    o_rows, logs = attend(q_rows, kv, own_kv, plan)
    attended_low = from_rows(o_rows).astype(BF16)

    middle = resid_in + dot(attended_low, out_w)
    normed_b, inv_b = norm_forward(middle, gain_b)
    normed_b_low = normed_b.astype(BF16)
    gate_pre = dot(normed_b_low, gate_w)
    up_pre = dot(normed_b_low, up_w)
    sigmoid_gate = jax.nn.sigmoid(gate_pre)
    silu_gate = gate_pre * sigmoid_gate
    hidden_low = (silu_gate * up_pre).astype(BF16)
    layer_out = middle + dot(hidden_low, down_w)

    grad_hidden = dot_nt(grad_low, down_w)
    grad_gate_pre = (
        grad_hidden * up_pre * sigmoid_gate * (1.0 + gate_pre * (1.0 - sigmoid_gate))
    ).astype(BF16)
    grad_up_pre = (grad_hidden * silu_gate).astype(BF16)
    grad_norm_b = dot_nt(grad_gate_pre, gate_w) + dot_nt(grad_up_pre, up_w)
    grad_mid_norm, grad_gain_b = norm_backward(middle, inv_b, gain_b, grad_norm_b)
    grad_middle = grad_low.astype(F32) + grad_mid_norm
    grad_branch = grad_middle.astype(BF16)
    do_rows = to_rows(dot_nt(grad_branch, out_w).astype(BF16))

    flat = reduce_grads(
        (
            (
                left_shards(normed_b_low, core),
                jnp.concatenate([grad_gate_pre, grad_up_pre], axis=1)[None],
            ),
            (grad_low.T[None], right_shards(hidden_low, core)),
            (left_shards(attended_low, core), pad_lanes(grad_branch)[None]),
        ),
        None,
        2,
    )
    shard_g, flat = unblock(flat, 240, 2560)
    shard_u, flat = unblock(flat, 240, 2560)
    shard_d, flat = unblock(flat, 960, 640)
    shard_o, _ = unblock(flat, 240, 960)

    dq_rows, dkv = attend_back(q_rows, do_rows, o_rows, logs, kv, own_kv, plan)
    dkv = scatter_kv(dkv, 3)
    dkv = dkv.T
    grad_value_low = dkv[:, 320:].astype(BF16)
    grad_key_pre = rotate(dkv[:, :320].reshape(TOK, KV_HEADS, HEAD), cosine, -sine)
    grad_query_pre = rotate(from_rows(dq_rows).reshape(TOK, HEADS, HEAD), cosine, -sine)
    grad_qkv = jnp.concatenate(
        [
            grad_query_pre.reshape(TOK, 960).astype(BF16),
            grad_key_pre.reshape(TOK, 320).astype(BF16),
            grad_value_low,
        ],
        axis=1,
    )
    grad_norm_a = dot_nt(grad_qkv, qkv_w)
    grad_in_norm, grad_gain_a = norm_backward(resid_in, inv_a, gain_a, grad_norm_a)
    grad_tokens = grad_middle + grad_in_norm

    gain_rows = jnp.stack([grad_gain_a, grad_gain_b]).reshape(2, 4, 240).transpose(1, 0, 2)
    gain_rows = jnp.pad(gain_rows, ((0, 0), (0, 0), (0, 16))).reshape(2, 2, 4, 128).astype(BF16)
    gain_rows = jnp.pad(gain_rows, ((0, 0), (0, 0), (0, 12), (0, 0)))
    flat = reduce_grads(
        ((left_shards(normed_a_low, core), pad_lanes(grad_qkv)[None]),),
        (pick(gain_rows, 1, core), pick(gain_rows, 1, 1 - core)),
        4,
    )
    shard_qkv, flat = unblock(flat, 240, 1600)
    shard_gains = flat[:4].reshape(2, 256)[:, :240].astype(F32)
    return (
        swap_rows(layer_out.astype(BF16), swap)[None],
        swap_rows(grad_tokens, swap)[None],
        shard_gains[0],
        shard_qkv[:, :960],
        shard_qkv[:, 960:1280],
        shard_qkv[:, 1280:],
        shard_o,
        shard_gains[1],
        shard_g,
        shard_u,
        shard_d.T,
    )


def solution(mesh):
    rows, cut = P("fsdp", "ctx", None), P("fsdp", None)
    return jax.shard_map(
        on_device,
        mesh=mesh,
        in_specs=(rows, rows, P(), P("fsdp"), cut, cut, cut, cut, P("fsdp"), cut, cut, cut),
        out_specs=(rows, rows, P("fsdp"), cut, cut, cut, cut, P("fsdp"), cut, cut, cut),
        check_vma=False,
    )
```

time: 1390 us -> 633 us (0.46); the launches traced: 1360 us -> 632 us
  waiting for transfers between devices: 906 us -> 0 us
  Pallas kernels: 0 us -> 507 us
  matrix products: 189 us -> 32.8 us
  blocking collectives: 69.2 us -> 0 us
  local copies, waits for them, and re-layouts: 138 us -> 71.2 us
  other arithmetic: 41.4 us -> 15.7 us
    pallas_call x0 -> x7, Pallas kernels: none -> 507 us  [the longest x2 161 us: reduce_grads(): pl.pallas_call(functools.partial(reduce_kernel, tuple(shapes), used, pa,...]
    all_gather x4 -> x0, waiting for transfers between devices: 317 us -> none  [the longest x1 139 us: sent_together(): result, at, done = (lax.all_gather(both, axis, axis=dim, tiled=True), 0, [])]
    psum x1 -> x0, waiting for transfers between devices: 267 us -> none  [together(): subtotal = lax.psum(ravelled, axis)]
    reduce_scatter x2 -> x0, waiting for transfers between devices: 174 us -> none  [the longest x1 131 us: sent_together_2(): lax.psum_scatter(both, axis, scatter_dimension=dim, tiled=True)]
    dot_general x49 -> x10, matrix products: 189 us -> 32.8 us  [the longest x5 19.2 us: dot_nt(): lax.dot_general(a, b, (((1,), (1,)), ((), ())), preferred_element_type=F32)]
    unnamed x9 -> x0, waiting for transfers between devices: 149 us -> none
    psum x1 -> x0, blocking collectives: 69.2 us -> none  [together(): subtotal = lax.psum(ravelled, axis)]
    concatenate x3 -> x7, local copies, waits for them, and re-layouts: 31.2 us -> 3.78 us  [the longest x1 1.96 us: on_device(): qkv_shard = jnp.concatenate([w_query, w_key, w_value], axis=1)]
  transfers between devices with their start and end apart: 8 -> 0, of which waited for: 8 -> 0; matrix products, arithmetic and copies ran while one was open for 7% -> 0% of each run, Pallas kernels for 0% -> 0%
where the time goes in v1:
time: 633 us; the launch traced here: 632 us
  Pallas kernels  507 us (80%)
  local copies, waits for them, and re-layouts  71.2 us (11%)
  matrix products  32.8 us (5%)
  other arithmetic  15.7 us (2%)
    pallas_call x2, Pallas kernels, reduce_grads(): pl.pallas_call(functools.partial(reduce_kernel, tuple(shapes), used, pa,...  161 us
    pallas_call x1, Pallas kernels, gather_weights(): pl.pallas_call(functools.partial(gather_kernel, n), out_shape=[jax.ShapeD...  159 us
    pallas_call x1, Pallas kernels, attend_back(): pl.pallas_call(attend_back_kernel, grid=(KV_HEADS,), out_shape=[jax.Shape...  64.8 us
    pallas_call x1, Pallas kernels, gather_kv(): pl.pallas_call(kv_gather_kernel, out_shape=jax.ShapeDtypeStruct((4, 2, 4,...  42.8 us
    pallas_call x1, Pallas kernels, scatter_kv(): pl.pallas_call(kv_scatter_kernel, out_shape=jax.ShapeDtypeStruct((640, 12...  41.5 us
    pallas_call x1, Pallas kernels, attend(): pl.pallas_call(attend_kernel, grid=(KV_HEADS,), out_shape=[jax.ShapeDtype...  38.6 us
    dot_general x5, matrix products, dot_nt(): lax.dot_general(a, b, (((1,), (1,)), ((), ())), preferred_element_type=F32)  19.2 us
    unnamed x67, local copies, waits for them, and re-layouts  18.7 us

profile of v1, /device:TPU:1, one launch (start us, length us, event | category | flops | bytes accessed | tf_op | source)
XLA Modules:
  0.0 631.6 jit_solution(9117630282387715094)
XLA Ops:
  0.7 0.8 stack.19
  2.7 1.1 copy.161
  3.8 1.1 copy.162
  4.8 2.0 concatenate.97.refs_1_
  6.8 1.9 copy.163.refs_5_
  8.7 158.8 %gather_weights.1 = (bf16[64,256]{1,0:T(8,128)(2,1)}, bf16[960,1600]{1,0:T(8,128)(2,1)}, bf16[960,960]{1,0:T(8,128)(2,1)}, bf16[960,2560]{1,0:T(8,128)(2,1)}, bf...) custom-call(bf16[16,256]{1,0:T(8,128)(2,1)} %fusion.29.refs_0_, bf16[240,1600]{1,0:T(8,128)(2,1)} %concatenate.97.refs_1_, ...), custom_call_target="tpu_custom_call" | custom-call | tf_op jit(solution)/shard_map/gather_weights/pallas_call | solution.py:121
  171.4 3.4 fusion.21
  175.1 1.1 concatenate.100
  179.5 1.9 fusion.3
  181.4 2.2 rev.12
  184.2 0.9 reshape.294.q_ref
  187.3 42.8 %gather_kv.1 = bf16[4,2,4,640,128]{4,3,2,1,0:T(8,128)(2,1)} custom-call(bf16[640,128]{1,0:T(8,128)(2,1)} %copy-done.12), custom_call_target="tpu_custom_call" | custom-call | tf_op jit(solution)/shard_map/gather_kv/pallas_call | solution.py:184
  234.5 38.6 %attend.1 = (f32[5,192,128]{2,1,0:T(8,128)}, f32[5,192,128]{2,1,0:T(8,128)}) custom-call(bf16[5,192,128]{2,1,0:T(8,128)(2,1)} %reshape.294.q_ref, bf16[32,640,128]{2,1,0:T(8,128)(2,1)} %bitcast.154, bf16[640,128]{1,0:T(8,128)(2,1)} %copy-done.12, f32[33,128]{1,0:T(8,128)} %get-tuple-element.123.flag_ref, f32[33,128]{1,0:T(8,128)} %get-tuple-element.122.left_ref, ...), custom_call_target="tpu_custom_call" | custom-call | tf_op jit(solution)/shard_map/attend/pallas_call | solution.py:396
  273.1 1.4 reshape.302
  275.1 2.4 rev.13
  278.4 4.4 fusion.42
  282.7 4.4 fusion.43
  287.4 6.5 %multiply_convert_fusion = (bf16[128,2560]{1,0:T(8,128)(2,1)}, bf16[128,2560]{1,0:T(8,128)(2,1)}, bf16[128,2560]{1,0:T(8,128)(2,1)S(1)}) fusion(f32[128,2560]{1,0:T(8,128)} %fusion.42, f32[128,2560]{1,0:T(8,128)} %fusion.43, bf16[128,960]{1,0:T(8,128)(2,1)S(1)} %maximum_select_fusion.3, bf16[2560,960]{1,0:T(8,128)(2,1)} %get-tuple-element.27), kind=kOutput, calls=%fused_computation.1 | convolution fusion | flops 634060800 | bytes 9748480 | tf_op jit(solution)/shard_map/dot_general | solution.py:319
  293.9 0.9 fusion.1
  294.8 0.8 fusion.18
  295.6 1.8 copy.199
  297.4 0.9 copy.175
  298.3 4.3 fusion.44
  302.6 4.1 multiply_reduce_fusion
  308.0 1.4 convolution_convert_fusion
  309.3 1.2 reshape.303
  311.1 2.2 rev.14
  313.5 0.9 copy.177
  314.4 64.8 %attend_back.1 = (f32[5,192,128]{2,1,0:T(8,128)}, bf16[32,640,128]{2,1,0:T(8,128)(2,1)}) custom-call(bf16[5,192,128]{2,1,0:T(8,128)(2,1)} %reshape.294.q_ref, bf16[5,128,192]{2,1,0:T(8,128)(2,1)} %bitcast.184, bf16[5,192,128]{2,1,0:T(8,128)(2,1)} %copy-done.11, bf16[5,128,192]{2,1,0:T(8,128)(2,1)} %bitcast.185, f32[5,192,128]{2,1,0:T(8,128)} %get-tuple-element.23.o_ref, ...), custom_call_target="tpu_custom_call" | custom-call | tf_op jit(solution)/shard_map/attend_back/pallas_call | solution.py:490
  379.3 1.6 reshape.305
  381.5 2.5 rev.15
  384.6 0.8 multiply_sine_fusion.1
  385.4 0.8 bitcast_multiply_fusion
  386.3 1.2 copy.179
  387.5 1.3 reshape_reshape.6
  388.8 1.1 slice_negate_fusion
  389.9 0.8 maximum_multiply_fusion.1
  390.8 1.2 copy.180
  392.1 41.5 %scatter_kv.1 = f32[640,128]{1,0:T(8,128)} custom-call(bf16[4,2,4,640,128]{4,3,2,1,0:T(8,128)(2,1)} %bitcast.161), custom_call_target="tpu_custom_call" | custom-call | tf_op jit(solution)/shard_map/scatter_kv/pallas_call | solution.py:252
  433.6 1.1 copy.181
  435.5 3.0 fusion.14
  439.1 1.0 copy.200
  441.0 0.8 pad_bitcast_fusion.refs_2_
  442.6 40.5 %reduce_grads.2 = bf16[3328,128]{1,0:T(8,128)(2,1)} custom-call(bf16[2,240,128]{2,1,0:T(8,128)(2,1)} %get-tuple-element.116.refs_0_, bf16[2,240,128]{2,1,0:T(8,128)(2,1)} %get-tuple-element.115.refs_1_, bf16[1,128,1664]{2,1,0:T(8,128)(2,1)} %pad_bitcast_fusion.refs_2_, bf16[2,16,128]{2,1,0:T(8,128)(2,1)} %get-tuple-element.125.refs_3_, ...), custom_call_target="tpu_custom_call" | custom-call | tf_op jit(solution)/shard_map/reduce_grads/pallas_call | solution.py:719
  483.2 0.8 slice.174
  484.5 0.7 copy.189
  485.5 1.3 copy.201
  486.8 0.9 fusion.36
  488.0 0.7 dynamic-slice_bitcast_fusion.2
  488.8 1.2 maximum_bitcast_fusion.refs_2_
  490.0 0.8 copy.194.refs_3_
  491.2 0.9 copy.210
  492.1 0.9 copy.211
  493.0 0.7 dynamic-slice_bitcast_fusion
  494.5 120.0 %reduce_grads.3 = bf16[16384,128]{1,0:T(8,128)(2,1)} custom-call(bf16[2,240,128]{2,1,0:T(8,128)(2,1)} %get-tuple-element.114.refs_0_, bf16[2,240,128]{2,1,0:T(8,128)(2,1)} %get-tuple-element.113.refs_1_, bf16[1,128,5120]{2,1,0:T(8,128)(2,1)} %maximum_bitcast_fusion.refs_2_, bf16[1,960,128]{2,1,0:T(8,128)(2,1)} %copy.194.refs_3_, ...), custom_call_target="tpu_custom_call" | custom-call | tf_op jit(solution)/shard_map/reduce_grads/pallas_call | solution.py:719
  614.5 1.1 slice.182
  615.7 1.1 slice_convert_fusion.1
  616.7 3.9 fusion.35
  620.7 1.6 copy.196
  622.3 2.0 copy.202
  624.3 1.6 copy.197
  625.9 2.0 copy.203
  627.9 1.6 copy.198
  629.5 2.0 copy.204
  (154 shorter events, 22.8 us)
Async XLA Ops:
  0.6 6.1 copy-start.13
  8.7 158.9 %copy-start.14 = (bf16[1,128,960]{1,2,0:T(8,128)(2,1)S(1)}, bf16[1,128,960]{1,2,0:T(8,128)(2,1)}, u32[]{:S(2)}) copy-start(bf16[1,128,960]{1,2,0:T(8,128)(2,1)} %param.12) | copy-start | bytes 737284
  8.7 159.1 %copy-start.21 = (s32[64]{0:T(128)S(1)}, s32[64]{0:T(128)}, u32[]{:S(2)}) copy-start(s32[64]{0:T(128)} %param.14) | copy-start | bytes 772
  171.4 3.4 copy-start.16
  178.2 0.6 copy-start.22
  178.9 5.3 copy-start.18
  186.7 0.7 copy-start.12
  187.3 46.5 %copy-start.23 = (f32[1,128]{1,0:T(1,128)S(1)}, f32[1,128]{1,0:T(1,128)}, u32[]{:S(2)}) copy-start(f32[1,128]{1,0:T(1,128)} %constant.88.clone.1) | copy-start | bytes 1540
  273.1 4.6 copy-start
  277.7 5.0 copy-start.9
  282.7 4.4 copy-start.15
  287.3 6.6 %slice-start = ((s8[5242880]{0:T(1024)(128)(4,1)}), s8[4194304]{0:T(1024)(128)(4,1)S(1)}, s32[]{:S(2)}) async-start(s8[5242880]{0:T(1024)(128)(4,1)} %bitcast.159), calls=%async_computation | async-start | bytes 8388608
  287.4 6.5 %slice-start.1 = ((s8[5242880]{0:T(1024)(128)(4,1)}), s8[1048576]{0:T(1024)(128)(4,1)S(1)}, s32[]{:S(2)}) async-start(s8[5242880]{0:T(1024)(128)(4,1)} %bitcast.159), calls=%async_computation.1 | async-start | bytes 2097152
  293.9 0.9 copy-start.3
  294.8 2.6 copy-start.1
  298.3 4.3 copy-start.5
  306.7 0.5 copy-start.19
  307.3 0.7 copy-start.7
  313.5 0.9 copy-start.11
  434.7 0.7 copy-start.17
  435.5 3.0 copy-start.20
  483.2 1.4 slice-start.2
  486.8 1.9 copy-start.2
  487.6 1.1 copy-start.6
  487.8 3.1 copy-start.4
  490.8 2.2 copy-start.10
  490.8 2.9 copy-start.8

commit v2 on v1

--- a/solution.py
+++ b/solution.py
@@ -74,39 +74,42 @@
         return copy
 
 
-def gather_kernel(count, *refs):
-    ins, outs = refs[:count], refs[count : 2 * count]
-    send, recv, local = refs[2 * count :]
-    me = here()
+def start_gather(me, sems, local, arrays):
     f = me["yl"] * 2 + me["c"]
     near = device(me, yl=1 - me["yl"])
     far = device(me, yl=1 - me["yl"], yh=1 - me["yh"])
     mate = device(me, c=1 - me["c"])
-    across = (1 - me["yl"]) * 2 + me["c"]
-    greet((near, far, mate))
-    sems = Sems(send, recv)
     parts, kept, own = [], [], []
-    for i, (a, b) in enumerate(zip(ins, outs)):
+    for i, (a, b) in enumerate(arrays):
         rows = a.shape[0]
         first = rows // 32 * 16 if i % 2 else (rows + 31) // 32 * 16
-        first = max(first, 0)
-        spans = [(0, first, near), (first, rows - first, far)]
-        for lo, size, dev in spans:
+        for lo, size, dev in ((0, first, near), (first, rows - first, far)):
             if size:
                 src = a.at[pl.ds(lo, size)]
                 dst = b.at[pl.ds(pl.multiple_of(f * rows + lo, 16), size)]
                 parts.append((sems.push(src, dst, dev), b, rows, lo, size))
-    for i, (a, b) in enumerate(zip(ins, outs)):
+    for i, (a, b) in enumerate(arrays):
         rows = a.shape[0]
         dst = b.at[pl.ds(pl.multiple_of(f * rows, 16), rows)]
         kept.append(sems.push(a, dst, mate))
         copy = pltpu.make_async_copy(a, dst, local.at[i])
         copy.start()
         own.append(copy)
+    return parts, kept, own
+
+
+def relay_gather(me, sems, started):
+    parts, kept, _ = started
+    across = (1 - me["yl"]) * 2 + me["c"]
+    mate = device(me, c=1 - me["c"])
     for copy, b, rows, lo, size in parts:
         copy.wait_recv()
         span = b.at[pl.ds(pl.multiple_of(across * rows + lo, 16), size)]
         kept.append(sems.push(span, span, mate))
+
+
+def end_gather(started):
+    parts, kept, own = started
     for copy in own:
         copy.wait()
     for copy in kept:
@@ -115,20 +118,37 @@
         copy.wait_send()
 
 
+def gather_kernel(count, *refs):
+    arrays = list(zip(refs[:count], refs[count : 2 * count]))
+    send, recv, local = refs[2 * count :]
+    me = here()
+    flip = 1 - me["yl"]
+    greet((device(me, yl=flip), device(me, yl=flip, yh=1 - me["yh"]), device(me, c=1 - me["c"])))
+    sems = Sems(send, recv)
+    started = start_gather(me, sems, local, arrays)
+    relay_gather(me, sems, started)
+    end_gather(started)
+
+
+def gathered(arrays):
+    return [jax.ShapeDtypeStruct((4 * a.shape[0], *a.shape[1:]), a.dtype) for a in arrays]
+
+
 def gather_weights(arrays, collective_id):
     n = len(arrays)
-    copies = 5 * n
     return pl.pallas_call(
         functools.partial(gather_kernel, n),
-        out_shape=[jax.ShapeDtypeStruct((4 * a.shape[0], *a.shape[1:]), a.dtype) for a in arrays],
-        in_specs=[ANY] * n,
+        out_shape=gathered(arrays),
+        in_specs=[VM] * n,
         out_specs=[ANY] * n,
         scratch_shapes=[
-            pltpu.SemaphoreType.DMA((copies,)),
-            pltpu.SemaphoreType.DMA((copies,)),
+            pltpu.SemaphoreType.DMA((5 * n,)),
+            pltpu.SemaphoreType.DMA((5 * n,)),
             pltpu.SemaphoreType.DMA((n,)),
         ],
-        compiler_params=pltpu.CompilerParams(collective_id=collective_id, has_side_effects=True),
+        compiler_params=pltpu.CompilerParams(
+            collective_id=collective_id, has_side_effects=True, vmem_limit_bytes=BIG
+        ),
         name="gather_weights",
     )(*arrays)
 
@@ -137,63 +157,34 @@
     return [(d, lax.rem(me[axis] + d, 4)) for d in (1, 3, 2)]
 
 
-def kv_gather_kernel(kv, out, send, recv, local):
-    me = here()
+def gather_kv(me, sems, kv, out):
     x, yh, z = me["x"], me["yh"], me["z"]
     other = device(me, yh=1 - yh)
-    xs = [(at, device(me, x=at)) for _, at in around(me, "x")]
-    zs = [(at, device(me, z=at)) for _, at in around(me, "z")]
-    greet([other] + [d for _, d in xs] + [d for _, d in zs])
-    sems = Sems(send, recv)
+    xs = [device(me, x=at) for _, at in around(me, "x")]
+    zs = [device(me, z=at) for _, at in around(me, "z")]
     key, value = pl.ds(0, 320), pl.ds(320, 320)
-    mine = pltpu.make_async_copy(kv, out.at[z, yh, x], local.at[0])
-    mine.start()
-    done = []
+    step2 = {}
+    step2[0, 0] = [sems.push(kv.at[key], out.at[z, yh, x, key], dev) for dev in xs]
+    step2[1, 0] = [sems.push(kv.at[value], out.at[z, yh, x, value], dev) for dev in zs]
     step1 = [sems.push(kv.at[p], out.at[z, yh, x, p], other) for p in (key, value)]
-    step2 = {(0, 0): [], (0, 1): [], (1, 0): [], (1, 1): []}
-    for _, dev in xs:
-        step2[0, 0].append(sems.push(kv.at[key], out.at[z, yh, x, key], dev))
-    for _, dev in zs:
-        step2[1, 0].append(sems.push(kv.at[value], out.at[z, yh, x, value], dev))
-    for axis, (devs, p) in enumerate(((xs, key), (zs, value))):
-        step1[axis].wait_recv()
-        span = out.at[z, 1 - yh, x, p]
-        for _, dev in devs:
-            step2[axis, 1].append(sems.push(span, span, dev))
-    mine.wait()
+    out[z, yh, x] = kv[...]
     step3 = []
     for hop in (0, 1):
         row = yh if hop == 0 else 1 - yh
-        for c in step2[0, hop]:
-            c.wait_recv()
-        span = out.at[z, row, :, key]
-        for _, dev in zs:
-            step3.append(sems.push(span, span, dev))
-        for c in step2[1, hop]:
-            c.wait_recv()
-        span = out.at[:, row, x, value]
-        for _, dev in xs:
-            step3.append(sems.push(span, span, dev))
+        for axis, (devs, p) in enumerate(((zs, key), (xs, value))):
+            for c in step2[axis, hop]:
+                c.wait_recv()
+            span = out.at[z, row, :, key] if axis == 0 else out.at[:, row, x, value]
+            for dev in devs:
+                step3.append(sems.push(span, span, dev))
+        if hop == 0:
+            for axis, (devs, p) in enumerate(((xs, key), (zs, value))):
+                step1[axis].wait_recv()
+                span = out.at[z, 1 - yh, x, p]
+                step2[axis, 1] = [sems.push(span, span, dev) for dev in devs]
     for c in step3:
         c.wait_recv()
-    for c in step1 + sum(step2.values(), []) + step3:
-        c.wait_send()
-
-
-def gather_kv(kv, collective_id):
-    return pl.pallas_call(
-        kv_gather_kernel,
-        out_shape=jax.ShapeDtypeStruct((4, 2, 4, 640, 128), BF16),
-        in_specs=[ANY],
-        out_specs=ANY,
-        scratch_shapes=[
-            pltpu.SemaphoreType.DMA((26,)),
-            pltpu.SemaphoreType.DMA((26,)),
-            pltpu.SemaphoreType.DMA((1,)),
-        ],
-        compiler_params=pltpu.CompilerParams(collective_id=collective_id, has_side_effects=True),
-        name="gather_kv",
-    )(kv).reshape(CTX, 640, 128)
+    return step1 + sum(step2.values(), []) + step3
 
 
 def kv_scatter_kernel(part, out, r1a, r1b, s1a, s1b, r2a, r2b, s2, r3, send, recv):
@@ -307,7 +298,7 @@
         tiles_ref[pl.ds(at, 128), :] = jnp.concatenate([top, low], axis=0).astype(BF16)
         return 0
 
-    lax.fori_loop(0, CTX, one, 0, unroll=4)
+    lax.fori_loop(0, CTX, one, 0, unroll=32)
     block = own_ref[pl.ds(start, HALF), :].astype(F32)
     top = jnp.where(lane < HALF, 0.0, pltpu.roll(block, HALF, 1))
     tiles_ref[pl.ds(CTX * 128, 128), :] = jnp.concatenate(
@@ -324,63 +315,46 @@
 
 
 ROWS = GROUP * HALF
-STEP = 3
+STEP = 33
 
 
 def row_offset():
     return lax.rem(lax.broadcasted_iota(jnp.int32, (ROWS, 128), 0), HALF).astype(F32)
 
 
-def attend_kernel(q_ref, kv_ref, own_ref, flag_ref, left_ref, limit_ref, o_ref, l_ref, kk, vv, s_ref):
-    head = pl.program_id(0)
+def attend_head(head, q, kv_ref, own_ref, flag_ref, left_ref, limit_ref, kk, vv):
     build_tiles(head, kv_ref, own_ref, left_ref, kk, 0)
     build_tiles(head, kv_ref, own_ref, left_ref, vv, 320)
-    q = q_ref[0]
     offset = row_offset()
     low = jnp.full((ROWS, 128), NEG, F32)
-
-    def scores(j, carry):
-        top_l, top_e = carry
-        at = pl.multiple_of(j * STEP * 128, 128)
-        s = dot_nt(q, kk[pl.ds(at, STEP * 128), :]) * (SCALE * LOG2E)
-        for t in range(STEP):
-            i = j * STEP + t
-            tile = s[:, t * 128 : (t + 1) * 128]
-            tile = jnp.where(limit_ref[pl.ds(i, 1), :] <= offset, tile, NEG)
-            late = flag_ref[pl.ds(i, 1), :] > 0.5
-            top_l = jnp.maximum(top_l, jnp.where(late, tile, NEG))
-            top_e = jnp.maximum(top_e, jnp.where(late, NEG, tile))
-            s_ref[:, pl.ds(pl.multiple_of(at + t * 128, 128), 128)] = tile
-        return top_l, top_e
-
-    top_l, top_e = lax.fori_loop(0, TILES // STEP, scores, (low, low))
+    s = dot_nt(q, kk[...]) * (SCALE * LOG2E)
+    tiles = []
+    top_l, top_e = low, low
+    for i in range(TILES):
+        tile = s[:, i * 128 : (i + 1) * 128]
+        tile = jnp.where(limit_ref[i : i + 1, :] <= offset, tile, NEG)
+        tiles.append(tile)
+        late = flag_ref[i : i + 1, :] > 0.5
+        top_l = jnp.maximum(top_l, jnp.where(late, tile, NEG))
+        top_e = jnp.maximum(top_e, jnp.where(late, NEG, tile))
     max_l = jnp.broadcast_to(jnp.max(top_l, axis=1, keepdims=True), (ROWS, 128))
     max_e = jnp.broadcast_to(jnp.max(top_e, axis=1, keepdims=True), (ROWS, 128))
-    zero = jnp.zeros((ROWS, 128), F32)
-
-    def values(j, carry):
-        sum_l, sum_e, total = carry
-        at = pl.multiple_of(j * STEP * 128, 128)
-        probs = []
-        for t in range(STEP):
-            i = j * STEP + t
-            tile = s_ref[:, pl.ds(pl.multiple_of(at + t * 128, 128), 128)]
-            late = flag_ref[pl.ds(i, 1), :] > 0.5
-            p = jnp.exp2(tile - jnp.where(late, max_l, max_e))
-            p_l = jnp.where(late, p, 0.0)
-            sum_l = sum_l + p_l
-            sum_e = sum_e + (p - p_l)
-            probs.append(p.astype(BF16))
-        total = total + dot_nn(jnp.concatenate(probs, axis=1), vv[pl.ds(at, STEP * 128), :])
-        return sum_l, sum_e, total
-
-    sum_l, sum_e, total = lax.fori_loop(0, TILES // STEP, values, (zero, zero, zero))
+    sum_l = jnp.zeros((ROWS, 128), F32)
+    sum_e = jnp.zeros((ROWS, 128), F32)
+    probs = []
+    for i in range(TILES):
+        late = flag_ref[i : i + 1, :] > 0.5
+        p = jnp.exp2(tiles[i] - jnp.where(late, max_l, max_e))
+        p_l = jnp.where(late, p, 0.0)
+        sum_l = sum_l + p_l
+        sum_e = sum_e + (p - p_l)
+        probs.append(p.astype(BF16))
+    total = dot_nn(jnp.concatenate(probs, axis=1), vv[...])
     late = lax.broadcasted_iota(jnp.int32, (ROWS, 128), 1) < HALF
     row_sum = jnp.where(
         late, jnp.sum(sum_l, axis=1, keepdims=True), jnp.sum(sum_e, axis=1, keepdims=True)
     )
-    o_ref[0] = total / row_sum
-    l_ref[0] = jnp.where(late, max_l, max_e) + jnp.log2(row_sum)
+    return total / row_sum, jnp.where(late, max_l, max_e) + jnp.log2(row_sum)
 
 
 def head_spec(*shape):
@@ -391,29 +365,66 @@
     return pl.BlockSpec(shape, lambda h: (0,) * len(shape))
 
 
-def attend(q, kv, own, plan):
+def forward_kernel(count, q_ref, own_ref, flag_ref, left_ref, limit_ref, *refs):
+    shards, refs = refs[:count], refs[count:]
+    o_ref, l_ref, kv_out, *full = refs[: 3 + count]
+    kv, kk, vv, send, recv, local = refs[3 + count :]
+    me = here()
+    flip = 1 - me["yl"]
+    greet(
+        [device(me, yl=flip), device(me, yl=flip, yh=1 - me["yh"]), device(me, c=1 - me["c"])]
+        + [device(me, yh=1 - me["yh"])]
+        + [device(me, x=at) for _, at in around(me, "x")]
+        + [device(me, z=at) for _, at in around(me, "z")]
+    )
+    sems = Sems(send, recv)
+    started = start_gather(me, sems, local, list(zip(shards, full)))
+    kv_copies = gather_kv(me, sems, own_ref, kv)
+    keep = pltpu.make_async_copy(kv, kv_out, local.at[count])
+    keep.start()
+    flat = kv.reshape(CTX, 640, 128)
+
+    def one(head, _):
+        o, logs = attend_head(
+            head, q_ref[head], flat, own_ref, flag_ref, left_ref, limit_ref, kk, vv
+        )
+        o_ref[head] = o
+        l_ref[head] = logs
+        return 0
+
+    lax.fori_loop(0, 3, one, 0)
+    relay_gather(me, sems, started)
+    lax.fori_loop(3, KV_HEADS, one, 0)
+    end_gather(started)
+    for copy in kv_copies:
+        copy.wait_send()
+    keep.wait()
+
+
+def forward(q, own, plan, shards, collective_id):
     flags, left, _, limits = plan
+    n = len(shards)
+    copies = 5 * n + 26
     return pl.pallas_call(
-        attend_kernel,
-        grid=(KV_HEADS,),
-        out_shape=[jax.ShapeDtypeStruct((KV_HEADS, ROWS, 128), F32)] * 2,
-        in_specs=[
-            head_spec(ROWS, 128),
-            whole_spec(CTX, 640, 128),
-            whole_spec(640, 128),
-            whole_spec(TILES, 128),
-            whole_spec(TILES, 128),
-            whole_spec(TILES, 128),
-        ],
-        out_specs=[head_spec(ROWS, 128)] * 2,
+        functools.partial(forward_kernel, n),
+        out_shape=[jax.ShapeDtypeStruct((KV_HEADS, ROWS, 128), F32)] * 2
+        + [jax.ShapeDtypeStruct((4, 2, 4, 640, 128), BF16)]
+        + gathered(shards),
+        in_specs=[VM] * (5 + n),
+        out_specs=[VM, VM, ANY] + [ANY] * n,
         scratch_shapes=[
+            pltpu.VMEM((4, 2, 4, 640, 128), BF16),
             pltpu.VMEM((KEYS, 128), BF16),
             pltpu.VMEM((KEYS, 128), BF16),
-            pltpu.VMEM((ROWS, KEYS), F32),
+            pltpu.SemaphoreType.DMA((copies,)),
+            pltpu.SemaphoreType.DMA((copies,)),
+            pltpu.SemaphoreType.DMA((n + 1,)),
         ],
-        compiler_params=pltpu.CompilerParams(vmem_limit_bytes=BIG),
-        name="attend",
-    )(q, kv, own, flags, left, limits)
+        compiler_params=pltpu.CompilerParams(
+            collective_id=collective_id, has_side_effects=True, vmem_limit_bytes=BIG
+        ),
+        name="forward",
+    )(q, own, flags, left, limits, *shards)
 
 
 def attend_back_kernel(
@@ -798,9 +809,7 @@
     core = lax.axis_index("fsdp") % 2
     gains = jnp.pad(jnp.stack([attn_gain, mlp_gain]), ((0, 14), (0, 16)))
     qkv_shard = jnp.concatenate([w_query, w_key, w_value], axis=1)
-    gains_all, qkv_w, out_w, gate_w, up_w, down_w = gather_weights(
-        (gains, qkv_shard, w_out, w_gate, w_up, w_down), 0
-    )
+    gains_all, qkv_w = gather_weights((gains, qkv_shard), 0)
     gains_all = gains_all.reshape(4, 16, 256)[:, :2, :240].astype(F32)
     gain_a = gains_all[:, 0].reshape(D)
     gain_b = gains_all[:, 1].reshape(D)
@@ -823,8 +832,10 @@
     keys = rotate(qkv[:, 960:1280].reshape(TOK, KV_HEADS, HEAD), cosine, sine).astype(BF16)
     q_rows = to_rows(queries)
     own_kv = jnp.concatenate([to_wire(keys), to_wire(value_low)], axis=0)
-    kv = gather_kv(own_kv, 1)
-    o_rows, logs = attend(q_rows, kv, own_kv, plan)
+    o_rows, logs, kv, out_w, gate_w, up_w, down_w = forward(
+        q_rows, own_kv, plan, (w_out, w_gate, w_up, w_down), 1
+    )
+    kv = kv.reshape(CTX, 640, 128)
     attended_low = from_rows(o_rows).astype(BF16)
 
     middle = resid_in + dot(attended_low, out_w)

time: 633 us -> 469 us (0.74); the launches traced: 632 us -> 461 us
  Pallas kernels: 507 us -> 337 us
    pallas_call x3 -> x2, Pallas kernels: 240 us -> 117 us  [the longest x1 98.5 us: forward(): pl.pallas_call(functools.partial(forward_kernel, n), out_shape=[jax.Shape...]
    pallas_call x1, Pallas kernels: 64.8 us -> 19.8 us  [attend_back(): pl.pallas_call(attend_back_kernel, grid=(KV_HEADS,), out_shape=[jax.Shape...]
    unnamed x67 -> x73, local copies, waits for them, and re-layouts: 18.7 us -> 18.6 us
where the time goes in v2:
time: 469 us; the launch traced here: 461 us
  Pallas kernels  337 us (72%)
  local copies, waits for them, and re-layouts  71.1 us (15%)
  matrix products  31.1 us (7%)
  other arithmetic  15.7 us (3%)
  between operations  5.33 us (1%)
    pallas_call x2, Pallas kernels, reduce_grads(): pl.pallas_call(functools.partial(reduce_kernel, tuple(shapes), used, pa,...  157 us
    pallas_call x1, Pallas kernels, forward(): pl.pallas_call(functools.partial(forward_kernel, n), out_shape=[jax.Shape...  98.5 us
    pallas_call x1, Pallas kernels, scatter_kv(): pl.pallas_call(kv_scatter_kernel, out_shape=jax.ShapeDtypeStruct((640, 12...  43.7 us
    dot_general x5, matrix products, dot_nt(): lax.dot_general(a, b, (((1,), (1,)), ((), ())), preferred_element_type=F32)  19.8 us
    pallas_call x1, Pallas kernels, attend_back(): pl.pallas_call(attend_back_kernel, grid=(KV_HEADS,), out_shape=[jax.Shape...  19.8 us
    unnamed x73, local copies, waits for them, and re-layouts  18.6 us
    pallas_call x1, Pallas kernels, gather_weights(): pl.pallas_call(functools.partial(gather_kernel, n), out_shape=gathered(ar...  18.1 us
    dot_general x5, matrix products, dot(): return jnp.dot(a, b, preferred_element_type=F32)  11.3 us

profile of v2, /device:TPU:1, one launch (start us, length us, event | category | flops | bytes accessed | tf_op | source)
XLA Modules:
  0.0 460.5 jit_solution(5787495063895664040)
XLA Ops:
  2.6 1.1 copy.161
  3.7 1.1 copy.162
  4.8 2.0 concatenate.97.refs_1_
  6.7 18.1 %gather_weights.1 = (bf16[64,256]{1,0:T(8,128)(2,1)}, bf16[960,1600]{1,0:T(8,128)(2,1)}) custom-call(bf16[16,256]{1,0:T(8,128)(2,1)} %fusion.29.refs_0_, bf16[240,1600]{1,0:T(8,128)(2,1)} %concatenate.97.refs_1_), custom_call_target="tpu_custom_call" | custom-call | tf_op jit(solution)/shard_map/gather_weights/pallas_call | solution.py:139
  27.8 0.7 slice_convert_fusion.4
  28.7 3.4 fusion.21
  32.4 1.1 concatenate.100
  36.2 1.9 fusion.3
  38.1 2.2 rev.12
  40.9 0.9 reshape.294.q_ref
  47.8 2.4 copy.166.refs_3_
  50.2 98.5 %forward.1 = (f32[5,192,128]{2,1,0:T(8,128)}, f32[5,192,128]{2,1,0:T(8,128)}, bf16[4,2,4,640,128]{4,3,2,1,0:T(8,128)(2,1)}, bf16[960,960]{1,0:T(8,128)(2,1)}, bf...) custom-call(bf16[5,192,128]{2,1,0:T(8,128)(2,1)} %reshape.294.q_ref, ...), custom_call_target="tpu_custom_call" | custom-call | tf_op jit(solution)/shard_map/forward/pallas_call | solution.py:408
  148.8 1.4 reshape.301
  150.7 2.2 rev.13
  153.9 4.5 fusion.42
  158.4 2.0 fusion.43
  160.7 6.5 %multiply_convert_fusion = (bf16[128,2560]{1,0:T(8,128)(2,1)}, bf16[128,2560]{1,0:T(8,128)(2,1)}, bf16[128,2560]{1,0:T(8,128)(2,1)S(1)}) fusion(f32[128,2560]{1,0:T(8,128)} %fusion.42, f32[128,2560]{1,0:T(8,128)} %fusion.43, bf16[128,960]{1,0:T(8,128)(2,1)S(1)} %maximum_select_fusion.3, bf16[2560,960]{1,0:T(8,128)(2,1)} %get-tuple-element.28), kind=kOutput, calls=%fused_computation.1 | convolution fusion | flops 634060800 | bytes 9748480 | tf_op jit(solution)/shard_map/dot_general | solution.py:310
  167.1 0.9 fusion.1
  168.1 0.8 fusion.18
  168.8 1.8 copy.199
  170.6 0.9 copy.175
  171.5 4.3 fusion.44
  175.8 4.7 %multiply_reduce_fusion = (bf16[960]{0:T(1024)(128)(2,1)}, f32[128]{0:T(128)S(1)}, f32[128,960]{1,0:T(8,128)S(1)}) fusion(f32[128,960]{1,0:T(8,128)S(1)} %get-tuple-element.139, f32[128]{0:T(128)S(1)} %add_rsqrt_fusion, f32[960]{0:T(1024)S(1)} %mul.317, f32[128,960]{1,0:T(8,128)S(1)} %fusion.44, bf16[128,2560]{1,0:T(8,128)(2,1)S(1)} %copy-done.6, ...), kind=kOutput, calls=%fused_computation.32 | convolution fusion | flops 630004672 | bytes 7051904 | tf_op jit(solution)/shard_map/dot_general | solution.py:310
  181.7 1.4 convolution_convert_fusion
  183.1 1.2 reshape.302
  184.8 2.4 rev.14
  187.5 0.9 copy.177
  188.4 19.8 %attend_back.1 = (f32[5,192,128]{2,1,0:T(8,128)}, bf16[32,640,128]{2,1,0:T(8,128)(2,1)}) custom-call(bf16[5,192,128]{2,1,0:T(8,128)(2,1)} %reshape.294.q_ref, bf16[5,128,192]{2,1,0:T(8,128)(2,1)} %bitcast.183, bf16[5,192,128]{2,1,0:T(8,128)(2,1)} %copy-done.12, bf16[5,128,192]{2,1,0:T(8,128)(2,1)} %bitcast.184, f32[5,192,128]{2,1,0:T(8,128)} %get-tuple-element.24.o_ref, ...), custom_call_target="tpu_custom_call" | custom-call | tf_op jit(solution)/shard_map/attend_back/pallas_call | solution.py:501
  208.2 1.6 reshape.305
  210.5 2.3 rev.15
  213.3 0.8 multiply_sine_fusion.1
  214.7 0.8 bitcast_multiply_fusion
  215.5 1.2 copy.179
  216.7 1.3 reshape_reshape.6
  218.1 1.1 slice_negate_fusion
  219.2 0.8 maximum_multiply_fusion.1
  220.0 1.2 copy.180
  221.3 43.7 %scatter_kv.1 = f32[640,128]{1,0:T(8,128)} custom-call(bf16[4,2,4,640,128]{4,3,2,1,0:T(8,128)(2,1)} %bitcast.157), custom_call_target="tpu_custom_call" | custom-call | tf_op jit(solution)/shard_map/scatter_kv/pallas_call | solution.py:243
  265.0 1.1 copy.181
  267.0 3.0 fusion.14
  270.6 1.0 copy.200
  272.5 0.8 pad_bitcast_fusion.refs_2_
  274.1 37.3 %reduce_grads.2 = bf16[3328,128]{1,0:T(8,128)(2,1)} custom-call(bf16[2,240,128]{2,1,0:T(8,128)(2,1)} %get-tuple-element.118.refs_0_, bf16[2,240,128]{2,1,0:T(8,128)(2,1)} %get-tuple-element.117.refs_1_, bf16[1,128,1664]{2,1,0:T(8,128)(2,1)} %pad_bitcast_fusion.refs_2_, bf16[2,16,128]{2,1,0:T(8,128)(2,1)} %get-tuple-element.127.refs_3_, ...), custom_call_target="tpu_custom_call" | custom-call | tf_op jit(solution)/shard_map/reduce_grads/pallas_call | solution.py:730
  311.4 0.7 slice.174
  312.8 1.0 copy.189
  314.0 1.3 copy.201
  315.3 0.9 fusion.36
  316.5 0.7 dynamic-slice_bitcast_fusion.2
  317.3 1.2 maximum_bitcast_fusion.refs_2_
  318.5 0.8 copy.194.refs_3_
  319.7 0.9 copy.210
  320.6 0.9 copy.211
  321.5 0.7 dynamic-slice_bitcast_fusion
  322.2 0.7 pad_bitcast_fusion.1.refs_8_
  323.0 120.0 %reduce_grads.3 = bf16[16384,128]{1,0:T(8,128)(2,1)} custom-call(bf16[2,240,128]{2,1,0:T(8,128)(2,1)} %get-tuple-element.116.refs_0_, bf16[2,240,128]{2,1,0:T(8,128)(2,1)} %get-tuple-element.115.refs_1_, bf16[1,128,5120]{2,1,0:T(8,128)(2,1)} %maximum_bitcast_fusion.refs_2_, bf16[1,960,128]{2,1,0:T(8,128)(2,1)} %copy.194.refs_3_, ...), custom_call_target="tpu_custom_call" | custom-call | tf_op jit(solution)/shard_map/reduce_grads/pallas_call | solution.py:730
  443.0 1.1 slice.182
  444.2 1.1 slice_convert_fusion.1
  445.3 3.9 fusion.35
  449.2 1.6 copy.196
  450.8 2.0 copy.202
  452.8 1.6 copy.197
  454.4 2.0 copy.203
  456.5 1.6 copy.198
  458.1 2.0 copy.204
  (159 shorter events, 21.4 us)
Async XLA Ops:
  0.6 24.2 %copy-start.16 = (bf16[1,128,960]{1,2,0:T(8,128)(2,1)S(1)}, bf16[1,128,960]{1,2,0:T(8,128)(2,1)}, u32[]{:S(2)}) copy-start(bf16[1,128,960]{1,2,0:T(8,128)(2,1)} %param.12) | copy-start | bytes 737284
  3.7 21.3 %copy-start.24 = (s32[64]{0:T(128)S(1)}, s32[64]{0:T(128)}, u32[]{:S(2)}) copy-start(s32[64]{0:T(128)} %param.14) | copy-start | bytes 772
  28.6 3.4 copy-start.19
  35.5 5.4 %copy-start.25 = (f32[128]{0:T(128)}, f32[128]{0:T(128)S(1)}, u32[]{:S(2)}) copy-start(f32[128]{0:T(128)S(1)} %add_convert_fusion.4) | copy-start | bytes 1540
  41.8 5.3 %copy-start.26 = (f32[1,128]{1,0:T(1,128)S(1)}, f32[1,128]{1,0:T(1,128)}, u32[]{:S(2)}) copy-start(f32[1,128]{1,0:T(1,128)} %constant.88.clone.1) | copy-start | bytes 1540
  43.4 6.8 %copy-start.13 = (bf16[640,128]{1,0:T(8,128)(2,1)}, bf16[640,128]{1,0:T(8,128)(2,1)S(1)}, u32[]{:S(2)}) copy-start(bf16[640,128]{1,0:T(8,128)(2,1)S(1)} %constant_dynamic-update-slice_fusion.own_ref) | copy-start | bytes 491524
  148.7 4.5 copy-start.1
  153.2 5.2 %copy-start.10 = (bf16[128,960]{0,1:T(8,128)(2,1)}, bf16[128,960]{0,1:T(8,128)(2,1)S(1)}, u32[]{:S(2)}) copy-start(bf16[128,960]{0,1:T(8,128)(2,1)S(1)} %convert_element_type.149) | copy-start | bytes 737284
  153.9 4.5 copy-start
  158.4 2.0 copy-start.17
  160.6 6.6 %slice-start = ((s8[5242880]{0:T(1024)(128)(4,1)}), s8[4194304]{0:T(1024)(128)(4,1)S(1)}, s32[]{:S(2)}) async-start(s8[5242880]{0:T(1024)(128)(4,1)} %bitcast.158), calls=%async_computation | async-start | bytes 8388608
  160.6 6.5 %slice-start.1 = ((s8[5242880]{0:T(1024)(128)(4,1)}), s8[1048576]{0:T(1024)(128)(4,1)S(1)}, s32[]{:S(2)}) async-start(s8[5242880]{0:T(1024)(128)(4,1)} %bitcast.158), calls=%async_computation.1 | async-start | bytes 2097152
  167.1 0.9 copy-start.4
  168.0 2.6 copy-start.2
  171.5 4.3 copy-start.6
  180.5 0.5 copy-start.22
  181.0 0.7 copy-start.8
  187.5 0.9 copy-start.12
  214.1 0.6 copy-start.14
  265.0 1.5 copy-start.15
  266.2 0.8 copy-start.20
  266.9 3.1 copy-start.21
  266.9 3.1 copy-start.23
  270.5 2.8 copy-start.18
  311.4 1.4 slice-start.2
  315.3 1.9 copy-start.3
  316.1 1.1 copy-start.7
  316.3 3.0 copy-start.5
  319.3 2.2 copy-start.11
  319.3 2.9 copy-start.9
